TPU v7x, 32 devices: a whole 2x2x4 slice. The times are simulated.
32 devices in a mesh: groups: 2 (over y), tm: 4 (over z), chan: 2 (over x), sub: 2 (over core).
Axes of the slice: x: 2, y: 2, z: 4, core: 2. Of those that a mesh axis runs over, the one named last changes fastest.
Arguments:
- signal: bfloat16 [2, 240, 65536], P(None, 'chan', ('groups', 'tm', 'sub')), parts along dimension 2, may hold values from -6 to 6
- channel_mask: int32 [240], P('chan'), may hold values from 0 to 1, as said below
- dispersion: float32 [240], P('chan'), may hold values from 1228.8 to 12288
- equaliser: bfloat16 [96, 2, 240, 240], P(('tm', 'chan')), may hold values from -0.25 to 0.25
- bin_block: int32 [64, 128], P(None, ('tm', 'chan')), may hold values from 0 to 11
Outputs:
- output: bfloat16 [2, 240, 65536], P(None, 'chan', ('groups', 'tm', 'sub')), parts along dimension 2
There are 2 independent parts, one for each index of `groups`. A program takes and returns all parts, laid end to end along the dimension named above; an argument that names none is the same for every part. Nothing has to cross between parts.
Inputs may be any that keep to these rules, and one draw needn't show every extreme that they name: `channel_mask`: exactly 228 entries are 1.
All inputs are finite; a program needn't handle non-finite values.
Results may differ from a plain program's by a relative error of at most 0.0089.
Values may be sent and summed in bfloat16 or wider, within the bound.
A program may use at most 128 MiB of HBM per device.

v0:
```python
import math

import jax
import jax.numpy as jnp
from jax import lax
from jax.sharding import PartitionSpec as P

TAPS = 4096
N1 = 128
NFFT = 8192
N2 = 64


def from_behind(value, axis, by):
    devices = lax.axis_size(axis)
    pairs = [(i, i + by) for i in range(devices) if 0 <= i + by < devices]
    return lax.ppermute(value, axis, pairs)


def dft_table(length, inverse):
    counter = jnp.arange(length, dtype=jnp.int32)
    product = counter[:, None] * counter[None, :] % length
    angle = product.astype(jnp.float32) * (2.0 * math.pi / length)
    factor = 1.0 / math.sqrt(length)
    cosine = jnp.cos(angle) * factor
    sine = jnp.sin(angle) * factor
    if inverse:
        upper = jnp.stack([cosine, -sine], axis=1)
        lower = jnp.stack([sine, cosine], axis=1)
    else:
        upper = jnp.stack([cosine, sine], axis=1)
        lower = jnp.stack([-sine, cosine], axis=1)
    return jnp.stack([upper, lower], axis=0).astype(jnp.bfloat16)


def twist_table(first_rows, columns):
    seconds = jnp.arange(columns, dtype=jnp.int32)
    product = first_rows[:, None] * seconds[None, :] % NFFT
    angle = product.astype(jnp.float32) * (2.0 * math.pi / NFFT)
    return (jnp.cos(angle), jnp.sin(angle))


def phase_table(dispersion):
    first_rows = jnp.arange(N1, dtype=jnp.int32)
    seconds = jnp.arange(N2, dtype=jnp.int32)
    bins = first_rows[:, None] + N1 * seconds[None, :]
    centred = jnp.where(bins < NFFT // 2, bins, bins - NFFT)
    freq_sq = (centred * centred).astype(jnp.float32) / float(NFFT * NFFT)
    quarter = jnp.mod(centred, 4).astype(jnp.float32) * (0.5 * math.pi)
    phase = dispersion[:, None, None] * freq_sq[None] - quarter[None]
    return (jnp.cos(phase), jnp.sin(phase))


def invert_second(spectra, first_rows, inverse_second):
    partial_value = jnp.einsum(
        "rspk,cjfpk->cjfrs", inverse_second, spectra, preferred_element_type=jnp.float32
    )
    cos_inv, sin_inv = twist_table(first_rows, N2)
    cos_inv = cos_inv[:, None, :]
    sin_inv = sin_inv[:, None, :]
    real_g = partial_value[:, :, :, 0]
    imag_g = partial_value[:, :, :, 1]
    turned = jnp.stack(
        [real_g * cos_inv - imag_g * sin_inv, imag_g * cos_inv + real_g * sin_inv], axis=3
    )
    return turned.astype(jnp.bfloat16)


def on_device(signal, channel_mask, dispersion, equaliser, bin_block):
    channels_dev = signal.shape[1]
    frame_count = signal.shape[2] // TAPS
    half_rows = N1 // 2
    mask_half = channel_mask.astype(jnp.bfloat16)
    masked = signal * mask_half[None, :, None]
    tail_in = from_behind(masked, ("tm", "sub"), 1)
    forward_first = dft_table(N1, False)
    forward_second = dft_table(N2, False)
    inverse_first = dft_table(N1, True)
    inverse_second = dft_table(N2, True)
    own_halves = masked.reshape(2, channels_dev, frame_count, TAPS)
    previous = jnp.concatenate([tail_in[:, :, None], own_halves[:, :, :-1]], axis=2)
    frames = jnp.concatenate([previous, own_halves], axis=3).reshape(
        2, channels_dev, frame_count, N1, N2
    )
    section_a = jnp.einsum(
        "pkqt,qcfts->cfpks", forward_first, frames, preferred_element_type=jnp.float32
    )
    cos_twist, sin_twist = twist_table(jnp.arange(N1, dtype=jnp.int32), N2)
    real_a = section_a[:, :, 0]
    imag_a = section_a[:, :, 1]
    twisted = jnp.stack(
        [real_a * cos_twist + imag_a * sin_twist, imag_a * cos_twist - real_a * sin_twist], axis=2
    ).astype(jnp.bfloat16)
    spectrum = jnp.einsum(
        "rlps,cfpks->ckfrl", forward_second, twisted, preferred_element_type=jnp.float32
    )
    cos_disp, sin_disp = phase_table(dispersion)
    cos_disp = cos_disp[:, :, None, :]
    sin_disp = sin_disp[:, :, None, :]
    real_s = spectrum[:, :, :, 0]
    imag_s = spectrum[:, :, :, 1]
    dispersed = jnp.stack(
        [real_s * cos_disp - imag_s * sin_disp, real_s * sin_disp + imag_s * cos_disp], axis=3
    )
    dispersed = dispersed.astype(jnp.bfloat16).reshape(channels_dev, N1, frame_count, 2 * N2)
    by_bins = lax.all_to_all(dispersed, ("tm", "chan"), split_axis=1, concat_axis=1, tiled=True)
    tm_count = lax.axis_size("tm")
    chan_count = lax.axis_size("chan")
    bins_rows = N1 // (tm_count * chan_count)
    grid = by_bins.reshape(channels_dev, tm_count, chan_count, bins_rows, frame_count, 2, N2)
    shaped_weights = equaliser.reshape(
        equaliser.shape[0], 2, chan_count, channels_dev, chan_count, channels_dev
    )
    group_size = 8

    def equalise_group(group_step, result):
        start = group_step * group_size
        columns = lax.dynamic_slice_in_dim(grid, start, group_size, 6)
        picks = lax.dynamic_slice_in_dim(bin_block, start, group_size, 0)
        chosen = jnp.take(shaped_weights, picks, axis=0)
        mixed = jnp.einsum(
            "gjsxyad,dtajfqg->ytxjfsqg", chosen, columns, preferred_element_type=jnp.float32
        )
        real_e = mixed[:, :, :, :, :, 0, 0] - mixed[:, :, :, :, :, 1, 1]
        imag_e = mixed[:, :, :, :, :, 0, 1] + mixed[:, :, :, :, :, 1, 0]
        block_out = jnp.stack([real_e, imag_e], axis=5).astype(jnp.bfloat16)
        return lax.dynamic_update_slice_in_dim(result, block_out, start, 6)

    equalised = lax.fori_loop(
        0, N2 // group_size, equalise_group, jnp.zeros(grid.shape, jnp.bfloat16)
    )
    equalised = equalised.reshape(channels_dev, N1, frame_count, 2, N2)
    returned = lax.all_to_all(
        equalised.reshape(channels_dev, N1, frame_count, 2 * N2),
        ("tm", "chan"),
        split_axis=1,
        concat_axis=1,
        tiled=True,
    )
    returned = returned.reshape(channels_dev, N1, frame_count, 2, N2)
    restored = invert_second(returned, jnp.arange(N1, dtype=jnp.int32), inverse_second)
    values = jnp.einsum(
        "rupj,cjfpt->rcfut",
        inverse_first[:, half_rows:],
        restored,
        preferred_element_type=jnp.float32,
    )
    values = values.reshape(2, channels_dev, frame_count * TAPS)
    return (values * channel_mask.astype(jnp.float32)[None, :, None]).astype(jnp.bfloat16)


def solution(mesh):
    in_specs = (
        P(None, "chan", ("groups", "tm", "sub")),
        P("chan"),
        P("chan"),
        P(("tm", "chan"), None, None, None),
        P(None, ("tm", "chan")),
    )
    out_specs = P(None, "chan", ("groups", "tm", "sub"))
    return jax.shard_map(
        on_device, mesh=mesh, in_specs=in_specs, out_specs=out_specs, check_vma=False
    )
```

profile of v0, /device:TPU:0, one launch (start us, length us, event | category | flops | bytes accessed | tf_op | source)
XLA Modules:
  0.0 997.1 jit_solution(6519776769160690254)
XLA Ops:
  11.1 7.1 copy.80
  23.8 7.2 copy.79
  39.8 15.6 %subtract_convert_fusion = (bf16[120,128,1,1,64]{1,4,3,0,2:T(8,128)(2,1)S(1)}, bf16[120,128,1,1,64]{1,4,3,0,2:T(8,128)(2,1)S(1)}) fusion(f32[120,128,1,2,64]{1,4,3,0,2:T(8,128)S(1)} %fusion.28, f32[128,64]{0,1:T(8,128)S(1)} %get-tuple-element.149, f32[128,64]{0,1:T(8,128)S(1)} %get-tuple-element.148, f32[120]{0:T(128)S(1)} %copy-done.9), kind=kLoop, calls=%fused_computation.50 | loop fusion | flops 9830400 | bytes 11862496 | tf_op jit(solution)/shard_map/convert.24
  64.2 17.3 %all-to-all-start = ((bf16[120,128,1,128]{3,0,2,1:T(8,128)(2,1)}), bf16[120,128,1,128]{3,0,2,1:T(8,128)(2,1)}, u32[]{:S(2)}, u32[]{:S(2)}) async-start(bf16[120,128,1,128]{3,0,2,1:T(8,128)(2,1)} %copy.86), calls=%async_computation | async-start | bytes 7864320 | tf_op jit(solution)/shard_map/all_to_all | solution.py:106
  87.9 79.5 %all-to-all-done = bf16[120,128,1,128]{3,0,2,1:T(8,128)(2,1)} async-done(((bf16[120,128,1,128]{3,0,2,1:T(8,128)(2,1)}), bf16[120,128,1,128]{3,0,2,1:T(8,128)(2,1)}, u32[]{:S(2)}, u32[]{:S(2)}) %all-to-all-start) | async-done | bytes 3932192 | tf_op jit(solution)/shard_map/all_to_all | solution.py:106
  176.8 692.4 %while.13 = (s32[]{:T(128)}, bf16[120,4,2,16,1,2,64]{0,6,5,3,2,1,4:T(8,128)(2,1)}, bf16[120,4,2,16,1,2,64]{0,6,5,3,2,1,4:T(8,128)(2,1)}, s32[64,16]{1,0:T(8,128)...) while((s32[]{:T(128)}, ...), condition=%wide.region_1.2_spmd, body=%wide.region_0.1_spmd.sunk | while | flops 251414272 | bytes 96378512 | solution.py:129
  178.1 64.6 %gather_fusion = bf16[128,2,2,120,2,120]{5,4,3,2,1,0:T(2,128)(2,1)} fusion(bf16[12,2,2,120,2,120]{5,4,3,2,1,0:T(2,128)(2,1)S(1)} %get-tuple-element.213, s32[1024]{0:T(1024)S(1)} %pad_clamp_fusion.2), kind=kCustom, calls=%fused_computation.clone.1 | custom fusion | bytes 58982912 | tf_op jit(solution)/shard_map/while/body/eval_jaxpr/jit(_take)/gather | solution.py:120
  242.7 19.0 %fusion.92 = f32[120,4,2,16,1,2,2,8]{0,1,2,5,6,7,3,4:T(4,128)S(1)} fusion(bf16[8,16,2,2,120,2,120]{6,5,4,3,2,1,0:T(2,128)(2,1)} %bitcast.201, pred[8,16]{0,1:T(8,128)(4,1)S(1)} %copy.146, bf16[120,4,2,16,1,2,8]{0,6,5,3,2,1,4:T(8,128)(2,1)S(1)} %constant_dynamic-slice_fusion.2), kind=kOutput, calls=%fused_computation.6.clone.1 | convolution fusion | flops 250675200 | bytes 31948928 | tf_op jit(solution)/shard_map/while/body/eval_jaxpr/gjsxyad,dtajfqg->ytxjfsqg/dot_general | solution.py:121
  264.6 64.7 %gather_fusion = bf16[128,2,2,120,2,120]{5,4,3,2,1,0:T(2,128)(2,1)} fusion(bf16[12,2,2,120,2,120]{5,4,3,2,1,0:T(2,128)(2,1)S(1)} %get-tuple-element.213, s32[1024]{0:T(1024)S(1)} %pad_clamp_fusion.2), kind=kCustom, calls=%fused_computation.clone.1 | custom fusion | bytes 58982912 | tf_op jit(solution)/shard_map/while/body/eval_jaxpr/jit(_take)/gather | solution.py:120
  329.3 19.0 %fusion.92 = f32[120,4,2,16,1,2,2,8]{0,1,2,5,6,7,3,4:T(4,128)S(1)} fusion(bf16[8,16,2,2,120,2,120]{6,5,4,3,2,1,0:T(2,128)(2,1)} %bitcast.201, pred[8,16]{0,1:T(8,128)(4,1)S(1)} %copy.146, bf16[120,4,2,16,1,2,8]{0,6,5,3,2,1,4:T(8,128)(2,1)S(1)} %constant_dynamic-slice_fusion.2), kind=kOutput, calls=%fused_computation.6.clone.1 | convolution fusion | flops 250675200 | bytes 31948928 | tf_op jit(solution)/shard_map/while/body/eval_jaxpr/gjsxyad,dtajfqg->ytxjfsqg/dot_general | solution.py:121
  351.2 64.7 %gather_fusion = bf16[128,2,2,120,2,120]{5,4,3,2,1,0:T(2,128)(2,1)} fusion(bf16[12,2,2,120,2,120]{5,4,3,2,1,0:T(2,128)(2,1)S(1)} %get-tuple-element.213, s32[1024]{0:T(1024)S(1)} %pad_clamp_fusion.2), kind=kCustom, calls=%fused_computation.clone.1 | custom fusion | bytes 58982912 | tf_op jit(solution)/shard_map/while/body/eval_jaxpr/jit(_take)/gather | solution.py:120
  415.9 19.0 %fusion.92 = f32[120,4,2,16,1,2,2,8]{0,1,2,5,6,7,3,4:T(4,128)S(1)} fusion(bf16[8,16,2,2,120,2,120]{6,5,4,3,2,1,0:T(2,128)(2,1)} %bitcast.201, pred[8,16]{0,1:T(8,128)(4,1)S(1)} %copy.146, bf16[120,4,2,16,1,2,8]{0,6,5,3,2,1,4:T(8,128)(2,1)S(1)} %constant_dynamic-slice_fusion.2), kind=kOutput, calls=%fused_computation.6.clone.1 | convolution fusion | flops 250675200 | bytes 31948928 | tf_op jit(solution)/shard_map/while/body/eval_jaxpr/gjsxyad,dtajfqg->ytxjfsqg/dot_general | solution.py:121
  437.8 64.6 %gather_fusion = bf16[128,2,2,120,2,120]{5,4,3,2,1,0:T(2,128)(2,1)} fusion(bf16[12,2,2,120,2,120]{5,4,3,2,1,0:T(2,128)(2,1)S(1)} %get-tuple-element.213, s32[1024]{0:T(1024)S(1)} %pad_clamp_fusion.2), kind=kCustom, calls=%fused_computation.clone.1 | custom fusion | bytes 58982912 | tf_op jit(solution)/shard_map/while/body/eval_jaxpr/jit(_take)/gather | solution.py:120
  502.4 19.0 %fusion.92 = f32[120,4,2,16,1,2,2,8]{0,1,2,5,6,7,3,4:T(4,128)S(1)} fusion(bf16[8,16,2,2,120,2,120]{6,5,4,3,2,1,0:T(2,128)(2,1)} %bitcast.201, pred[8,16]{0,1:T(8,128)(4,1)S(1)} %copy.146, bf16[120,4,2,16,1,2,8]{0,6,5,3,2,1,4:T(8,128)(2,1)S(1)} %constant_dynamic-slice_fusion.2), kind=kOutput, calls=%fused_computation.6.clone.1 | convolution fusion | flops 250675200 | bytes 31948928 | tf_op jit(solution)/shard_map/while/body/eval_jaxpr/gjsxyad,dtajfqg->ytxjfsqg/dot_general | solution.py:121
  524.3 64.7 %gather_fusion = bf16[128,2,2,120,2,120]{5,4,3,2,1,0:T(2,128)(2,1)} fusion(bf16[12,2,2,120,2,120]{5,4,3,2,1,0:T(2,128)(2,1)S(1)} %get-tuple-element.213, s32[1024]{0:T(1024)S(1)} %pad_clamp_fusion.2), kind=kCustom, calls=%fused_computation.clone.1 | custom fusion | bytes 58982912 | tf_op jit(solution)/shard_map/while/body/eval_jaxpr/jit(_take)/gather | solution.py:120
  589.0 19.0 %fusion.92 = f32[120,4,2,16,1,2,2,8]{0,1,2,5,6,7,3,4:T(4,128)S(1)} fusion(bf16[8,16,2,2,120,2,120]{6,5,4,3,2,1,0:T(2,128)(2,1)} %bitcast.201, pred[8,16]{0,1:T(8,128)(4,1)S(1)} %copy.146, bf16[120,4,2,16,1,2,8]{0,6,5,3,2,1,4:T(8,128)(2,1)S(1)} %constant_dynamic-slice_fusion.2), kind=kOutput, calls=%fused_computation.6.clone.1 | convolution fusion | flops 250675200 | bytes 31948928 | tf_op jit(solution)/shard_map/while/body/eval_jaxpr/gjsxyad,dtajfqg->ytxjfsqg/dot_general | solution.py:121
  611.0 64.7 %gather_fusion = bf16[128,2,2,120,2,120]{5,4,3,2,1,0:T(2,128)(2,1)} fusion(bf16[12,2,2,120,2,120]{5,4,3,2,1,0:T(2,128)(2,1)S(1)} %get-tuple-element.213, s32[1024]{0:T(1024)S(1)} %pad_clamp_fusion.2), kind=kCustom, calls=%fused_computation.clone.1 | custom fusion | bytes 58982912 | tf_op jit(solution)/shard_map/while/body/eval_jaxpr/jit(_take)/gather | solution.py:120
  675.6 19.0 %fusion.92 = f32[120,4,2,16,1,2,2,8]{0,1,2,5,6,7,3,4:T(4,128)S(1)} fusion(bf16[8,16,2,2,120,2,120]{6,5,4,3,2,1,0:T(2,128)(2,1)} %bitcast.201, pred[8,16]{0,1:T(8,128)(4,1)S(1)} %copy.146, bf16[120,4,2,16,1,2,8]{0,6,5,3,2,1,4:T(8,128)(2,1)S(1)} %constant_dynamic-slice_fusion.2), kind=kOutput, calls=%fused_computation.6.clone.1 | convolution fusion | flops 250675200 | bytes 31948928 | tf_op jit(solution)/shard_map/while/body/eval_jaxpr/gjsxyad,dtajfqg->ytxjfsqg/dot_general | solution.py:121
  697.5 64.5 %gather_fusion = bf16[128,2,2,120,2,120]{5,4,3,2,1,0:T(2,128)(2,1)} fusion(bf16[12,2,2,120,2,120]{5,4,3,2,1,0:T(2,128)(2,1)S(1)} %get-tuple-element.213, s32[1024]{0:T(1024)S(1)} %pad_clamp_fusion.2), kind=kCustom, calls=%fused_computation.clone.1 | custom fusion | bytes 58982912 | tf_op jit(solution)/shard_map/while/body/eval_jaxpr/jit(_take)/gather | solution.py:120
  762.0 19.0 %fusion.92 = f32[120,4,2,16,1,2,2,8]{0,1,2,5,6,7,3,4:T(4,128)S(1)} fusion(bf16[8,16,2,2,120,2,120]{6,5,4,3,2,1,0:T(2,128)(2,1)} %bitcast.201, pred[8,16]{0,1:T(8,128)(4,1)S(1)} %copy.146, bf16[120,4,2,16,1,2,8]{0,6,5,3,2,1,4:T(8,128)(2,1)S(1)} %constant_dynamic-slice_fusion.2), kind=kOutput, calls=%fused_computation.6.clone.1 | convolution fusion | flops 250675200 | bytes 31948928 | tf_op jit(solution)/shard_map/while/body/eval_jaxpr/gjsxyad,dtajfqg->ytxjfsqg/dot_general | solution.py:121
  783.9 64.7 %gather_fusion = bf16[128,2,2,120,2,120]{5,4,3,2,1,0:T(2,128)(2,1)} fusion(bf16[12,2,2,120,2,120]{5,4,3,2,1,0:T(2,128)(2,1)S(1)} %get-tuple-element.213, s32[1024]{0:T(1024)S(1)} %pad_clamp_fusion.2), kind=kCustom, calls=%fused_computation.clone.1 | custom fusion | bytes 58982912 | tf_op jit(solution)/shard_map/while/body/eval_jaxpr/jit(_take)/gather | solution.py:120
  848.6 19.0 %fusion.92 = f32[120,4,2,16,1,2,2,8]{0,1,2,5,6,7,3,4:T(4,128)S(1)} fusion(bf16[8,16,2,2,120,2,120]{6,5,4,3,2,1,0:T(2,128)(2,1)} %bitcast.201, pred[8,16]{0,1:T(8,128)(4,1)S(1)} %copy.146, bf16[120,4,2,16,1,2,8]{0,6,5,3,2,1,4:T(8,128)(2,1)S(1)} %constant_dynamic-slice_fusion.2), kind=kOutput, calls=%fused_computation.6.clone.1 | convolution fusion | flops 250675200 | bytes 31948928 | tf_op jit(solution)/shard_map/while/body/eval_jaxpr/gjsxyad,dtajfqg->ytxjfsqg/dot_general | solution.py:121
  875.6 91.4 %all_to_all.10 = bf16[120,128,1,128]{3,0,2,1:T(8,128)(2,1)} all-to-all(bf16[120,128,1,128]{3,0,2,1:T(8,128)(2,1)} %copy.91), channel_id=1, replica_groups=mesh['groups'=2,'tm'=4,'chan'=2,'sub'=2] {'tm','chan'}, dimensions={1} | all-to-all | bytes 7864320 | tf_op jit(solution)/shard_map/all_to_all | solution.py:133
  983.4 8.5 copy.98
  (127 shorter events, 101.1 us)
Async XLA Ops:
  4.3 16.4 %collective-permute-start = (bf16[2,120,4096]{2,1,0:T(8,128)(2,1)}, bf16[2,120,4096]{2,1,0:T(8,128)(2,1)}, u32[]{:S(2)}, u32[]{:S(2)}) collective-permute-start(bf16[2,120,4096]{2,1,0:T(8,128)(2,1)} %broadcast_multiply_fusion), channel_id=1, source_target_pairs={{0,1},{1,4},{4,5},{5,8},{8,9},{9,12},{12,13},{2,3},{3,6},{6,7},{7,... | collective-permute-start | bytes 5898248 | tf_op jit(solution)/shard_map/ppermute | solution.py:17
  19.0 18.6 %copy-start = (f32[128,64]{0,1:T(8,128)}, f32[128,64]{0,1:T(8,128)S(1)}, u32[]{:S(2)}) copy-start(f32[128,64]{0,1:T(8,128)S(1)} %get-tuple-element.152) | copy-start | bytes 98308
  19.0 18.6 %copy-start.2 = (f32[128,64]{0,1:T(8,128)}, f32[128,64]{0,1:T(8,128)S(1)}, u32[]{:S(2)}) copy-start(f32[128,64]{0,1:T(8,128)S(1)} %get-tuple-element.153) | copy-start | bytes 98308
  38.6 1.2 copy-start.9
  64.2 17.3 %copy-start.8 = (s32[64,16]{0,1:T(8,128)S(1)}, s32[64,16]{0,1:T(8,128)}, u32[]{:S(2)}) copy-start(s32[64,16]{0,1:T(8,128)} %param.11) | copy-start | bytes 12292
  64.2 103.3 %all-to-all-start = ((bf16[120,128,1,128]{3,0,2,1:T(8,128)(2,1)}), bf16[120,128,1,128]{3,0,2,1:T(8,128)(2,1)}, u32[]{:S(2)}, u32[]{:S(2)}) async-start(bf16[120,128,1,128]{3,0,2,1:T(8,128)(2,1)} %copy.86), calls=%async_computation | async-start | bytes 7864320 | tf_op jit(solution)/shard_map/all_to_all | solution.py:106
  967.0 6.7 copy-start.6
  967.0 6.7 copy-start.7
  973.6 3.4 copy-start.1
  973.6 3.4 copy-start.3
  978.0 1.0 copy-start.4
  978.0 1.0 copy-start.5
  983.4 8.5 copy-start.10
where the time goes:
time: 999 us; the launch traced here: 997 us
  local copies, waits for them, and re-layouts  601 us (60%)
  matrix products  166 us (17%)
  blocking collectives  91.4 us (9%)
  waiting for transfers between devices  79.6 us (8%)
  other arithmetic  37.1 us (4%)
  starting transfers between devices  20.9 us (2%)
    gather x8, local copies, waits for them, and re-layouts, equalise_group(): chosen = jnp.take(shaped_weights, picks, axis=0)  517 us
    dot_general x8, matrix products, equalise_group(): jnp.einsum('gjsxyad,dtajfqg->ytxjfsqg', chosen, columns, preferred_elemen...  152 us
    all_to_all x1, blocking collectives, on_device(): lax.all_to_all(equalised.reshape(channels_dev, N1, frame_count, 2 * N2),...  91.4 us
    all_to_all x1, waiting for transfers between devices, on_device(): lax.all_to_all(dispersed, ('tm', 'chan'), split_axis=1, concat_axis=1, ti...  79.5 us
  transfers between devices with their start and end apart: 2, of which 1 were waited for; matrix products, arithmetic and copies ran while one was open for 2% of the time, Pallas kernels for 0%

commit v1 on v0

--- a/solution.py
+++ b/solution.py
@@ -3,6 +3,8 @@
 import jax
 import jax.numpy as jnp
 from jax import lax
+from jax.experimental import pallas as pl
+from jax.experimental.pallas import tpu as pltpu
 from jax.sharding import PartitionSpec as P
 
 TAPS = 4096
@@ -53,7 +55,7 @@
 
 def invert_second(spectra, first_rows, inverse_second):
     partial_value = jnp.einsum(
-        "rspk,cjfpk->cjfrs", inverse_second, spectra, preferred_element_type=jnp.float32
+        "rspk,jfcpk->cjfrs", inverse_second, spectra, preferred_element_type=jnp.float32
     )
     cos_inv, sin_inv = twist_table(first_rows, N2)
     cos_inv = cos_inv[:, None, :]
@@ -64,6 +66,44 @@
         [real_g * cos_inv - imag_g * sin_inv, imag_g * cos_inv + real_g * sin_inv], axis=3
     )
     return turned.astype(jnp.bfloat16)
+
+
+def equalise_kernel(picks_ref, weights_ref, columns_ref, out_ref):
+    values = columns_ref[0].astype(jnp.float32)
+    channels, width = values.shape
+    chosen = jnp.broadcast_to(picks_ref[...], values.shape)
+    mixed = jnp.zeros((2 * channels, width), jnp.float32)
+    for block in range(weights_ref.shape[0]):
+        part = jnp.where(chosen == block, values, 0.0).astype(jnp.bfloat16)
+        mixed = mixed + jnp.dot(
+            weights_ref[block], part, preferred_element_type=jnp.float32
+        )
+    lane = lax.broadcasted_iota(jnp.int32, (channels, 2 * N2), 1)
+    for start in range(0, width, 2 * N2):
+        by_real = mixed[:channels, start : start + 2 * N2]
+        by_imag = pltpu.roll(mixed[channels:, start : start + 2 * N2], N2, 1)
+        turned = by_real + jnp.where(lane < N2, -by_imag, by_imag)
+        out_ref[0, :, start : start + 2 * N2] = turned.astype(jnp.bfloat16)
+
+
+def equalise(columns, equaliser, picks):
+    frames, channels, lanes = columns.shape
+    blocks = equaliser.shape[0]
+    width = math.gcd(lanes, 8 * N2)
+    weights = equaliser.reshape(blocks, 2 * channels, channels)
+    spec = pl.BlockSpec((1, channels, width), lambda m, i: (m, 0, i))
+    return pl.pallas_call(
+        equalise_kernel,
+        grid=(frames, lanes // width),
+        in_specs=[
+            pl.BlockSpec((1, width), lambda m, i: (0, i)),
+            pl.BlockSpec((blocks, 2 * channels, channels), lambda m, i: (0, 0, 0)),
+            spec,
+        ],
+        out_specs=spec,
+        out_shape=jax.ShapeDtypeStruct(columns.shape, jnp.bfloat16),
+        compiler_params=pltpu.CompilerParams(vmem_limit_bytes=40 * 1024 * 1024),
+    )(picks, weights, columns)
 
 
 def on_device(signal, channel_mask, dispersion, equaliser, bin_block):
@@ -92,52 +132,34 @@
         [real_a * cos_twist + imag_a * sin_twist, imag_a * cos_twist - real_a * sin_twist], axis=2
     ).astype(jnp.bfloat16)
     spectrum = jnp.einsum(
-        "rlps,cfpks->ckfrl", forward_second, twisted, preferred_element_type=jnp.float32
+        "rlps,cfpks->kfcrl", forward_second, twisted, preferred_element_type=jnp.float32
     )
     cos_disp, sin_disp = phase_table(dispersion)
-    cos_disp = cos_disp[:, :, None, :]
-    sin_disp = sin_disp[:, :, None, :]
+    cos_disp = jnp.swapaxes(cos_disp, 0, 1)[:, None]
+    sin_disp = jnp.swapaxes(sin_disp, 0, 1)[:, None]
     real_s = spectrum[:, :, :, 0]
     imag_s = spectrum[:, :, :, 1]
-    dispersed = jnp.stack(
+    dispersed = jnp.concatenate(
         [real_s * cos_disp - imag_s * sin_disp, real_s * sin_disp + imag_s * cos_disp], axis=3
-    )
-    dispersed = dispersed.astype(jnp.bfloat16).reshape(channels_dev, N1, frame_count, 2 * N2)
-    by_bins = lax.all_to_all(dispersed, ("tm", "chan"), split_axis=1, concat_axis=1, tiled=True)
+    ).astype(jnp.bfloat16)
+    by_bins = lax.all_to_all(dispersed, ("tm", "chan"), split_axis=0, concat_axis=0, tiled=True)
     tm_count = lax.axis_size("tm")
     chan_count = lax.axis_size("chan")
     bins_rows = N1 // (tm_count * chan_count)
-    grid = by_bins.reshape(channels_dev, tm_count, chan_count, bins_rows, frame_count, 2, N2)
-    shaped_weights = equaliser.reshape(
-        equaliser.shape[0], 2, chan_count, channels_dev, chan_count, channels_dev
+    grid = by_bins.reshape(tm_count, chan_count, bins_rows, frame_count, channels_dev, 2 * N2)
+    columns = jnp.transpose(grid, (0, 3, 1, 4, 2, 5)).reshape(
+        tm_count * frame_count, chan_count * channels_dev, bins_rows * 2 * N2
     )
-    group_size = 8
-
-    def equalise_group(group_step, result):
-        start = group_step * group_size
-        columns = lax.dynamic_slice_in_dim(grid, start, group_size, 6)
-        picks = lax.dynamic_slice_in_dim(bin_block, start, group_size, 0)
-        chosen = jnp.take(shaped_weights, picks, axis=0)
-        mixed = jnp.einsum(
-            "gjsxyad,dtajfqg->ytxjfsqg", chosen, columns, preferred_element_type=jnp.float32
-        )
-        real_e = mixed[:, :, :, :, :, 0, 0] - mixed[:, :, :, :, :, 1, 1]
-        imag_e = mixed[:, :, :, :, :, 0, 1] + mixed[:, :, :, :, :, 1, 0]
-        block_out = jnp.stack([real_e, imag_e], axis=5).astype(jnp.bfloat16)
-        return lax.dynamic_update_slice_in_dim(result, block_out, start, 6)
-
-    equalised = lax.fori_loop(
-        0, N2 // group_size, equalise_group, jnp.zeros(grid.shape, jnp.bfloat16)
+    picks = jnp.broadcast_to(bin_block.T[:, None, :], (bins_rows, 2, N2)).reshape(1, -1)
+    equalised = equalise(columns, equaliser, picks)
+    equalised = equalised.reshape(
+        tm_count, frame_count, chan_count, channels_dev, bins_rows, 2 * N2
     )
-    equalised = equalised.reshape(channels_dev, N1, frame_count, 2, N2)
-    returned = lax.all_to_all(
-        equalised.reshape(channels_dev, N1, frame_count, 2 * N2),
-        ("tm", "chan"),
-        split_axis=1,
-        concat_axis=1,
-        tiled=True,
+    equalised = jnp.transpose(equalised, (0, 2, 4, 1, 3, 5)).reshape(
+        N1, frame_count, channels_dev, 2 * N2
     )
-    returned = returned.reshape(channels_dev, N1, frame_count, 2, N2)
+    returned = lax.all_to_all(equalised, ("tm", "chan"), split_axis=0, concat_axis=0, tiled=True)
+    returned = returned.reshape(N1, frame_count, channels_dev, 2, N2)
     restored = invert_second(returned, jnp.arange(N1, dtype=jnp.int32), inverse_second)
     values = jnp.einsum(
         "rupj,cjfpt->rcfut",

time: 999 us -> 335 us (0.34)
  local copies, waits for them, and re-layouts: 601 us -> 61.3 us
  matrix products: 166 us -> 14.4 us
  Pallas kernels: 0 us -> 29.8 us
    gather x8 -> x0, local copies, waits for them, and re-layouts: 517 us -> none  [equalise_group(): chosen = jnp.take(shaped_weights, picks, axis=0)]
    dot_general x10 -> x2, matrix products: 156 us -> 4.56 us  [the longest x1 3.33 us: invert_second(): jnp.einsum('rspk,jfcpk->cjfrs', inverse_second, spectra, preferred_elemen...]
    pallas_call x0 -> x1, Pallas kernels: none -> 29.8 us  [equalise(): pl.pallas_call(equalise_kernel, grid=(frames, lanes // width), in_specs=[...]
    another operation x30 -> x4, other arithmetic: 24.6 us -> 0.85 us
    concatenate x0 -> x2, other arithmetic: none -> 17.9 us  [on_device(): jnp.concatenate([real_s * cos_disp - imag_s * sin_disp, real_s * sin_disp...]
  transfers between devices with their start and end apart: 2 -> 2, of which waited for: 1 -> 1; matrix products, arithmetic and copies ran while one was open for 2% -> 3% of each run, Pallas kernels for 0% -> 0%
where the time goes in v1:
time: 335 us; the launch traced here: 334 us
  blocking collectives  91.2 us (27%)
  waiting for transfers between devices  85.9 us (26%)
  local copies, waits for them, and re-layouts  61.3 us (18%)
  Pallas kernels  29.8 us (9%)
  other arithmetic  29.3 us (9%)
  starting transfers between devices  22.2 us (7%)
  matrix products  14.4 us (4%)
    all_to_all x1, blocking collectives, on_device(): lax.all_to_all(equalised, ('tm', 'chan'), split_axis=0, concat_axis=0, ti...  91.2 us
    all_to_all x1, waiting for transfers between devices, on_device(): lax.all_to_all(dispersed, ('tm', 'chan'), split_axis=0, concat_axis=0, ti...  85.9 us
    pallas_call x1, Pallas kernels, equalise(): pl.pallas_call(equalise_kernel, grid=(frames, lanes // width), in_specs=[...  29.8 us
    all_to_all x1, starting transfers between devices, on_device(): lax.all_to_all(dispersed, ('tm', 'chan'), split_axis=0, concat_axis=0, ti...  18.6 us
    concatenate x2, other arithmetic, on_device(): jnp.concatenate([real_s * cos_disp - imag_s * sin_disp, real_s * sin_disp...  17.9 us
    concatenate x2, local copies, waits for them, and re-layouts, on_device(): jnp.concatenate([previous, own_halves], axis=3)  14.3 us
    transpose x1, local copies, waits for them, and re-layouts, on_device(): jnp.einsum('rupj,cjfpt->rcfut', inverse_first[:, half_rows:], restored, p...  8.53 us
    reshape x1, local copies, waits for them, and re-layouts, on_device(): jnp.transpose(grid, (0, 3, 1, 4, 2, 5))  7.25 us
  transfers between devices with their start and end apart: 2, of which 1 were waited for; matrix products, arithmetic and copies ran while one was open for 3% of the time, Pallas kernels for 0%

profile of v1, /device:TPU:0, one launch (start us, length us, event | category | flops | bytes accessed | tf_op | source)
XLA Modules:
  0.0 334.3 jit_solution(9063288281754454909)
XLA Ops:
  0.7 3.0 broadcast_multiply_fusion
  3.7 3.7 %collective-permute-start = (bf16[2,120,4096]{2,1,0:T(8,128)(2,1)}, bf16[2,120,4096]{2,1,0:T(8,128)(2,1)}, u32[]{:S(2)}, u32[]{:S(2)}) collective-permute-start(bf16[2,120,4096]{2,1,0:T(8,128)(2,1)} %broadcast_multiply_fusion), channel_id=1, source_target_pairs={{0,1},{1,4},{4,5},{5,8},{8,9},{9,12},{12,13},{2,3},{3,6},{6,7},{7,... | collective-permute-start | bytes 5898248 | tf_op jit(solution)/shard_map/ppermute | solution.py:19
  7.4 3.1 copy.62
  10.5 7.1 %copy.64 = bf16[2,120,1,64,64]{3,4,0,1,2:T(8,128)(2,1)} copy(bf16[2,120,1,64,64]{1,4,3,0,2:T(8,128)(2,1)S(1)} %bitcast.197) | data formatting | bytes 3932160 | tf_op jit(solution)/shard_map/concatenate | solution.py:122
  18.8 3.1 copy.61
  22.0 7.1 %copy.63 = bf16[2,120,1,64,64]{3,4,0,1,2:T(8,128)(2,1)} copy(bf16[2,120,1,64,64]{1,4,3,0,2:T(8,128)(2,1)S(1)} %bitcast.196) | data formatting | bytes 3932160 | tf_op jit(solution)/shard_map/concatenate | solution.py:122
  29.1 5.5 %fusion.21 = f32[120,1,2,128,64]{3,4,2,0,1:T(8,128)S(1)} fusion(bf16[2,120,1,64,64]{3,4,0,1,2:T(8,128)(2,1)} %copy.64, bf16[2,120,1,64,64]{3,4,0,1,2:T(8,128)(2,1)} %copy.63, bf16[1,128,2,128]{3,1,2,0:T(8,128)(2,1)S(1)} %get-tuple-element.8, bf16[1,128,2,128]{3,1,2,0:T(8,128)(2,1)S(1)} %get-tuple-element.11), kind=kOutput, calls=%fused_computation.35 | convolution fusion | flops 1014759424 | bytes 11927552 | tf_op jit(solution)/shard_map/pkqt,qcfts->cfpks/dot_general | solution.py:125
  37.9 15.6 %fusion.26 = (bf16[128,1,120,64]{0,3,2,1:T(8,128)(2,1)S(1)}, bf16[128,1,120,64]{0,3,2,1:T(8,128)(2,1)S(1)}) fusion(f32[128,1,120,2,64]{0,4,3,2,1:T(8,128)S(1)} %fusion.15, f32[128,64]{0,1:T(8,128)S(1)} %get-tuple-element.22, f32[128,64]{0,1:T(8,128)S(1)} %get-tuple-element.21, f32[120]{0:T(128)S(1)} %copy-done.3), kind=kLoop, calls=%fused_computation.41 | loop fusion | flops 9830400 | bytes 11862496 | tf_op jit(solution)/shard_map/concatenate | solution.py:142
  53.6 2.2 pad_maximum_fusion
  55.8 6.6 %copy.71 = bf16[128,1,120,128]{3,2,1,0:T(8,128)(2,1)} copy(bf16[128,1,120,128]{0,3,2,1:T(8,128)(2,1)} %pad_maximum_fusion) | data formatting | bytes 7864320 | tf_op jit(solution)/shard_map/concatenate | solution.py:142
  62.3 18.6 %all-to-all-start = ((bf16[128,1,120,128]{3,2,1,0:T(8,128)(2,1)}), bf16[128,1,120,128]{3,2,1,0:T(8,128)(2,1)}, u32[]{:S(2)}, u32[]{:S(2)}) async-start(bf16[128,1,120,128]{3,2,1,0:T(8,128)(2,1)} %copy.71), calls=%async_computation | async-start | bytes 7864320 | tf_op jit(solution)/shard_map/all_to_all | solution.py:145
  81.0 85.9 %all-to-all-done = bf16[128,1,120,128]{3,2,1,0:T(8,128)(2,1)} async-done(((bf16[128,1,120,128]{3,2,1,0:T(8,128)(2,1)}), bf16[128,1,120,128]{3,2,1,0:T(8,128)(2,1)}, u32[]{:S(2)}, u32[]{:S(2)}) %all-to-all-start) | async-done | bytes 3932192 | tf_op jit(solution)/shard_map/all_to_all | solution.py:145
  166.9 4.6 %copy.72 = bf16[4,1,2,120,16,128]{5,4,3,2,0,1:T(8,128)(2,1)} copy(bf16[4,1,2,120,16,128]{5,3,4,2,0,1:T(8,128)(2,1)} %bitcast.34) | data formatting | bytes 7864320 | tf_op jit(solution)/shard_map/transpose | solution.py:150
  171.6 7.3 %reshape.471.columns_ref = bf16[4,240,2048]{2,1,0:T(8,128)(2,1)} reshape(bf16[4,1,2,120,16,128]{5,4,3,2,0,1:T(8,128)(2,1)} %copy.72) | data formatting | bytes 7864320 | tf_op jit(solution)/shard_map/reshape | solution.py:150
  178.8 2.1 copy-done
  180.9 29.8 %shard_map.55 = bf16[4,240,2048]{2,1,0:T(8,128)(2,1)S(1)} custom-call(s32[1,2048]{1,0:T(1,128)S(1)} %reshape.467.picks_ref, bf16[12,480,240]{2,1,0:T(8,128)(2,1)S(1)} %bitcast.191, bf16[4,240,2048]{2,1,0:T(8,128)(2,1)S(1)} %copy-done), custom_call_target="tpu_custom_call" | custom-call | tf_op jit(solution)/shard_map/pallas_call | solution.py:95
  210.8 1.3 copy.98
  213.1 91.2 %all_to_all.10 = bf16[128,1,120,128]{3,2,1,0:T(8,128)(2,1)} all-to-all(bf16[128,1,120,128]{3,2,1,0:T(8,128)(2,1)S(1)} %bitcast.195), channel_id=1, replica_groups=mesh['groups'=2,'tm'=4,'chan'=2,'sub'=2] {'tm','chan'}, dimensions={0} | all-to-all | bytes 7864320 | tf_op jit(solution)/shard_map/all_to_all | solution.py:161
  304.3 6.7 %copy.75 = bf16[128,1,120,128]{0,3,2,1:T(8,128)(2,1)} copy(bf16[128,1,120,128]{3,2,1,0:T(8,128)(2,1)} %all_to_all.10) | data formatting | bytes 7864320 | tf_op jit(solution)/shard_map/all_to_all | solution.py:161
  311.0 3.3 convolution_bitcast_fusion
  316.3 4.3 %fusion.18 = f32[2,120,1,64,64]{3,4,0,1,2:T(8,128)} fusion(bf16[1,128,2,128]{3,1,2,0:T(8,128)(2,1)S(1)} %get-tuple-element.12, bf16[1,128,2,128]{3,1,2,0:T(8,128)(2,1)S(1)} %get-tuple-element.7, bf16[120,128,1,64]{1,3,0,2:T(8,128)(2,1)S(1)} %fusion.25, bf16[120,128,1,64]{1,3,0,2:T(8,128)(2,1)S(1)} %fusion.24), kind=kOutput, calls=%fused_computation.34 | convolution fusion | flops 505413632 | bytes 7995392 | tf_op jit(solution)/shard_map/rupj,cjfpt->rcfut/dot_general | solution.py:164
  320.6 8.5 %copy.81 = f32[2,120,1,64,64]{1,4,3,0,2:T(8,128)} copy(f32[2,120,1,64,64]{3,4,0,1,2:T(8,128)} %fusion.18) | data formatting | bytes 7864320 | tf_op jit(solution)/shard_map/rupj,cjfpt->rcfut/transpose | solution.py:164
  329.1 2.5 multiply_convert_fusion
  331.6 2.7 copy.82
  (26 shorter events, 8.2 us)
Async XLA Ops:
  3.7 15.1 %collective-permute-start = (bf16[2,120,4096]{2,1,0:T(8,128)(2,1)}, bf16[2,120,4096]{2,1,0:T(8,128)(2,1)}, u32[]{:S(2)}, u32[]{:S(2)}) collective-permute-start(bf16[2,120,4096]{2,1,0:T(8,128)(2,1)} %broadcast_multiply_fusion), channel_id=1, source_target_pairs={{0,1},{1,4},{4,5},{5,8},{8,9},{9,12},{12,13},{2,3},{3,6},{6,7},{7,... | collective-permute-start | bytes 5898248 | tf_op jit(solution)/shard_map/ppermute | solution.py:19
  36.7 1.2 copy-start.3
  62.3 18.6 %copy-start.2 = (s32[64,16]{0,1:T(8,128)S(1)}, s32[64,16]{0,1:T(8,128)}, u32[]{:S(2)}) copy-start(s32[64,16]{0,1:T(8,128)} %param.9) | copy-start | bytes 12292
  62.3 104.6 %all-to-all-start = ((bf16[128,1,120,128]{3,2,1,0:T(8,128)(2,1)}), bf16[128,1,120,128]{3,2,1,0:T(8,128)(2,1)}, u32[]{:S(2)}, u32[]{:S(2)}) async-start(bf16[128,1,120,128]{3,2,1,0:T(8,128)(2,1)} %copy.71), calls=%async_computation | async-start | bytes 7864320 | tf_op jit(solution)/shard_map/all_to_all | solution.py:145
  171.6 7.3 %copy-start.1 = (bf16[12,2,240,240]{3,2,1,0:T(8,128)(2,1)S(1)}, bf16[12,2,240,240]{3,2,1,0:T(8,128)(2,1)}, u32[]{:S(2)}) copy-start(bf16[12,2,240,240]{3,2,1,0:T(8,128)(2,1)} %param.8) | copy-start | bytes 8294404
  178.8 2.1 copy-start

commit v2 on v1

--- a/solution.py
+++ b/solution.py
@@ -1,3 +1,4 @@
+import functools
 import math
 
 import jax
@@ -68,59 +69,62 @@
     return turned.astype(jnp.bfloat16)
 
 
-def equalise_kernel(picks_ref, weights_ref, columns_ref, out_ref):
-    values = columns_ref[0].astype(jnp.float32)
-    channels, width = values.shape
+def equalise_kernel(parts, picks_ref, weights_ref, *refs):
+    out_ref = refs[parts]
+    shares = refs[0].shape[1]
+    pieces = [refs[part][0, share] for share in range(shares) for part in range(parts)]
+    values = jnp.concatenate([piece.astype(jnp.float32) for piece in pieces], axis=0)
+    width = values.shape[1]
+    outputs = out_ref.shape[1]
     chosen = jnp.broadcast_to(picks_ref[...], values.shape)
-    mixed = jnp.zeros((2 * channels, width), jnp.float32)
+    mixed = jnp.zeros((2 * outputs, width), jnp.float32)
     for block in range(weights_ref.shape[0]):
         part = jnp.where(chosen == block, values, 0.0).astype(jnp.bfloat16)
         mixed = mixed + jnp.dot(
             weights_ref[block], part, preferred_element_type=jnp.float32
         )
-    lane = lax.broadcasted_iota(jnp.int32, (channels, 2 * N2), 1)
+    lane = lax.broadcasted_iota(jnp.int32, (outputs, 2 * N2), 1)
     for start in range(0, width, 2 * N2):
-        by_real = mixed[:channels, start : start + 2 * N2]
-        by_imag = pltpu.roll(mixed[channels:, start : start + 2 * N2], N2, 1)
+        by_real = mixed[:outputs, start : start + 2 * N2]
+        by_imag = pltpu.roll(mixed[outputs:, start : start + 2 * N2], N2, 1)
         turned = by_real + jnp.where(lane < N2, -by_imag, by_imag)
         out_ref[0, :, start : start + 2 * N2] = turned.astype(jnp.bfloat16)
 
 
-def equalise(columns, equaliser, picks):
-    frames, channels, lanes = columns.shape
-    blocks = equaliser.shape[0]
+def equalise(columns, weights, picks):
+    frames, _, _, lanes = columns[0].shape
+    blocks, rows, channels = weights.shape
+    outputs = rows // 2
     width = math.gcd(lanes, 8 * N2)
-    weights = equaliser.reshape(blocks, 2 * channels, channels)
-    spec = pl.BlockSpec((1, channels, width), lambda m, i: (m, 0, i))
+    flops = 2 * frames * lanes * blocks * rows * channels
+    moved = 2 * (weights.size + frames * lanes * (channels + outputs))
     return pl.pallas_call(
-        equalise_kernel,
+        functools.partial(equalise_kernel, len(columns)),
         grid=(frames, lanes // width),
         in_specs=[
             pl.BlockSpec((1, width), lambda m, i: (0, i)),
-            pl.BlockSpec((blocks, 2 * channels, channels), lambda m, i: (0, 0, 0)),
-            spec,
+            pl.BlockSpec((blocks, rows, channels), lambda m, i: (0, 0, 0)),
+        ]
+        + [
+            pl.BlockSpec((1,) + part.shape[1:3] + (width,), lambda m, i: (m, 0, 0, i))
+            for part in columns
         ],
-        out_specs=spec,
-        out_shape=jax.ShapeDtypeStruct(columns.shape, jnp.bfloat16),
+        out_specs=pl.BlockSpec((1, outputs, width), lambda m, i: (m, 0, i)),
+        out_shape=jax.ShapeDtypeStruct((frames, outputs, lanes), jnp.bfloat16),
+        cost_estimate=pl.CostEstimate(flops=flops, bytes_accessed=moved, transcendentals=0),
         compiler_params=pltpu.CompilerParams(vmem_limit_bytes=40 * 1024 * 1024),
-    )(picks, weights, columns)
-
-
-def on_device(signal, channel_mask, dispersion, equaliser, bin_block):
-    channels_dev = signal.shape[1]
+    )(picks, weights, *columns)
+
+
+def to_bins(signal, channel_mask, dispersion, forward_first, forward_second):
+    channels = signal.shape[1]
     frame_count = signal.shape[2] // TAPS
-    half_rows = N1 // 2
-    mask_half = channel_mask.astype(jnp.bfloat16)
-    masked = signal * mask_half[None, :, None]
-    tail_in = from_behind(masked, ("tm", "sub"), 1)
-    forward_first = dft_table(N1, False)
-    forward_second = dft_table(N2, False)
-    inverse_first = dft_table(N1, True)
-    inverse_second = dft_table(N2, True)
-    own_halves = masked.reshape(2, channels_dev, frame_count, TAPS)
+    masked = signal * channel_mask.astype(jnp.bfloat16)[None, :, None]
+    tail_in = from_behind(masked[:, :, -TAPS:], ("tm", "sub"), 1)
+    own_halves = masked.reshape(2, channels, frame_count, TAPS)
     previous = jnp.concatenate([tail_in[:, :, None], own_halves[:, :, :-1]], axis=2)
     frames = jnp.concatenate([previous, own_halves], axis=3).reshape(
-        2, channels_dev, frame_count, N1, N2
+        2, channels, frame_count, N1, N2
     )
     section_a = jnp.einsum(
         "pkqt,qcfts->cfpks", forward_first, frames, preferred_element_type=jnp.float32
@@ -139,36 +143,67 @@
     sin_disp = jnp.swapaxes(sin_disp, 0, 1)[:, None]
     real_s = spectrum[:, :, :, 0]
     imag_s = spectrum[:, :, :, 1]
-    dispersed = jnp.concatenate(
+    return jnp.concatenate(
         [real_s * cos_disp - imag_s * sin_disp, real_s * sin_disp + imag_s * cos_disp], axis=3
     ).astype(jnp.bfloat16)
-    by_bins = lax.all_to_all(dispersed, ("tm", "chan"), split_axis=0, concat_axis=0, tiled=True)
+
+
+def from_bins(returned, channel_mask, inverse_first, inverse_second):
+    _, frame_count, channels, _ = returned.shape
+    returned = returned.reshape(N1, frame_count, channels, 2, N2)
+    restored = invert_second(returned, jnp.arange(N1, dtype=jnp.int32), inverse_second)
+    values = jnp.einsum(
+        "rupj,cjfpt->rcfut",
+        inverse_first[:, N1 // 2 :],
+        restored,
+        preferred_element_type=jnp.float32,
+    )
+    values = values.reshape(2, channels, frame_count * TAPS)
+    return (values * channel_mask.astype(jnp.float32)[None, :, None]).astype(jnp.bfloat16)
+
+
+def on_device(signal, channel_mask, dispersion, equaliser, bin_block):
+    channels_dev = signal.shape[1]
+    frame_count = signal.shape[2] // TAPS
     tm_count = lax.axis_size("tm")
     chan_count = lax.axis_size("chan")
     bins_rows = N1 // (tm_count * chan_count)
-    grid = by_bins.reshape(tm_count, chan_count, bins_rows, frame_count, channels_dev, 2 * N2)
-    columns = jnp.transpose(grid, (0, 3, 1, 4, 2, 5)).reshape(
-        tm_count * frame_count, chan_count * channels_dev, bins_rows * 2 * N2
-    )
+    first = -(-channels_dev // 16) * 8
+    parts = ((0, first), (first, channels_dev))
+    forward = (dft_table(N1, False), dft_table(N2, False))
+    inverse = (dft_table(N1, True), dft_table(N2, True))
+    columns = []
+    for low, high in parts:
+        dispersed = to_bins(
+            signal[:, low:high], channel_mask[low:high], dispersion[low:high], *forward
+        )
+        by_bins = lax.all_to_all(
+            dispersed, ("tm", "chan"), split_axis=0, concat_axis=0, tiled=True
+        )
+        grid = by_bins.reshape(tm_count, chan_count, bins_rows, frame_count, high - low, 2 * N2)
+        columns.append(
+            jnp.transpose(grid, (0, 3, 1, 4, 2, 5)).reshape(
+                tm_count * frame_count, chan_count, high - low, bins_rows * 2 * N2
+            )
+        )
     picks = jnp.broadcast_to(bin_block.T[:, None, :], (bins_rows, 2, N2)).reshape(1, -1)
-    equalised = equalise(columns, equaliser, picks)
-    equalised = equalised.reshape(
-        tm_count, frame_count, chan_count, channels_dev, bins_rows, 2 * N2
-    )
-    equalised = jnp.transpose(equalised, (0, 2, 4, 1, 3, 5)).reshape(
-        N1, frame_count, channels_dev, 2 * N2
-    )
-    returned = lax.all_to_all(equalised, ("tm", "chan"), split_axis=0, concat_axis=0, tiled=True)
-    returned = returned.reshape(N1, frame_count, channels_dev, 2, N2)
-    restored = invert_second(returned, jnp.arange(N1, dtype=jnp.int32), inverse_second)
-    values = jnp.einsum(
-        "rupj,cjfpt->rcfut",
-        inverse_first[:, half_rows:],
-        restored,
-        preferred_element_type=jnp.float32,
-    )
-    values = values.reshape(2, channels_dev, frame_count * TAPS)
-    return (values * channel_mask.astype(jnp.float32)[None, :, None]).astype(jnp.bfloat16)
+    blocks, _, _, channels = equaliser.shape
+    weights = equaliser.reshape(blocks, 2, chan_count, channels_dev, channels)
+    results = []
+    for low, high in parts:
+        rows = 2 * chan_count * (high - low)
+        mine = weights[:, :, :, low:high].reshape(blocks, rows, channels)
+        equalised = equalise(columns, mine, picks).reshape(
+            tm_count, frame_count, chan_count, high - low, bins_rows, 2 * N2
+        )
+        equalised = jnp.transpose(equalised, (0, 2, 4, 1, 3, 5)).reshape(
+            N1, frame_count, high - low, 2 * N2
+        )
+        returned = lax.all_to_all(
+            equalised, ("tm", "chan"), split_axis=0, concat_axis=0, tiled=True
+        )
+        results.append(from_bins(returned, channel_mask[low:high], *inverse))
+    return jnp.concatenate(results, axis=1)
 
 
 def solution(mesh):

time: 335 us -> 315 us (0.940)
  blocking collectives: 91.2 us -> 0 us
  starting transfers between devices: 22.2 us -> 61.3 us
  local copies, waits for them, and re-layouts: 61.3 us -> 77.2 us
  waiting for transfers between devices: 85.9 us -> 100 us
  Pallas kernels: 29.8 us -> 34.3 us
    all_to_all x1 -> x0, blocking collectives: 91.2 us -> none  [on_device(): lax.all_to_all(equalised, ('tm', 'chan'), split_axis=0, concat_axis=0, ti...]
    all_to_all x0 -> x2, waiting for transfers between devices: none -> 50.9 us  [on_device(): lax.all_to_all(equalised, ('tm', 'chan'), split_axis=0, concat_axis=0, ti...]
    all_to_all x1 -> x2, waiting for transfers between devices: 85.9 us -> 49.2 us  [on_device(): lax.all_to_all(dispersed, ('tm', 'chan'), split_axis=0, concat_axis=0, ti...]
    all_to_all x1 -> x2, starting transfers between devices: 18.6 us -> 46.8 us  [on_device(): lax.all_to_all(dispersed, ('tm', 'chan'), split_axis=0, concat_axis=0, ti...]
    concatenate x3 -> x10, local copies, waits for them, and re-layouts: 20.8 us -> 30.4 us  [the longest x8 24.8 us: to_bins(): jnp.concatenate([previous, own_halves], axis=3)]
    reshape x1 -> x4, local copies, waits for them, and re-layouts: 1.01 us -> 10.2 us  [the longest x2 6.67 us: from_bins(): values = values.reshape(2, channels, frame_count * TAPS)]
    all_to_all x0 -> x2, starting transfers between devices: none -> 8.88 us  [on_device(): lax.all_to_all(equalised, ('tm', 'chan'), split_axis=0, concat_axis=0, ti...]
    pallas_call x1 -> x2, Pallas kernels: 29.8 us -> 34.3 us  [equalise(): pl.pallas_call(functools.partial(equalise_kernel, len(columns)), grid=(fr...]
  transfers between devices with their start and end apart: 2 -> 6, of which waited for: 1 -> 4; matrix products, arithmetic and copies ran while one was open for 3% -> 21% of each run, Pallas kernels for 0% -> 6%
where the time goes in v2:
time: 315 us; the launch traced here: 314 us
  waiting for transfers between devices  100 us (32%)
  local copies, waits for them, and re-layouts  77.2 us (25%)
  starting transfers between devices  61.3 us (19%)
  Pallas kernels  34.3 us (11%)
  other arithmetic  26.5 us (8%)
  matrix products  14 us (4%)
    all_to_all x2, waiting for transfers between devices, on_device(): lax.all_to_all(equalised, ('tm', 'chan'), split_axis=0, concat_axis=0, ti...  50.9 us
    all_to_all x2, waiting for transfers between devices, on_device(): lax.all_to_all(dispersed, ('tm', 'chan'), split_axis=0, concat_axis=0, ti...  49.2 us
    all_to_all x2, starting transfers between devices, on_device(): lax.all_to_all(dispersed, ('tm', 'chan'), split_axis=0, concat_axis=0, ti...  46.8 us
    pallas_call x2, Pallas kernels, equalise(): pl.pallas_call(functools.partial(equalise_kernel, len(columns)), grid=(fr...  34.3 us
    concatenate x8, local copies, waits for them, and re-layouts, to_bins(): jnp.concatenate([previous, own_halves], axis=3)  24.8 us
    concatenate x4, other arithmetic, to_bins(): jnp.concatenate([real_s * cos_disp - imag_s * sin_disp, real_s * sin_disp...  16.4 us
    transpose x2, local copies, waits for them, and re-layouts, from_bins(): jnp.einsum('rupj,cjfpt->rcfut', inverse_first[:, N1 // 2:], restored, pre...  11 us
    all_to_all x2, starting transfers between devices, on_device(): lax.all_to_all(equalised, ('tm', 'chan'), split_axis=0, concat_axis=0, ti...  8.88 us
  transfers between devices with their start and end apart: 6, of which 4 were waited for; matrix products, arithmetic and copies ran while one was open for 21% of the time, Pallas kernels for 6%

profile of v2, /device:TPU:0, one launch (start us, length us, event | category | flops | bytes accessed | tf_op | source)
XLA Modules:
  0.0 313.8 jit_solution(5902068111347602755)
XLA Ops:
  2.0 3.3 %collective-permute-start.1 = (bf16[2,56,4096]{2,1,0:T(8,128)(2,1)S(1)}, bf16[2,56,4096]{2,1,0:T(8,128)(2,1)}, u32[]{:S(2)}, u32[]{:S(2)}) collective-permute-start(bf16[2,56,4096]{2,1,0:T(8,128)(2,1)S(1)} %slice_multiply_fusion.1), channel_id=1, source_target_pairs={{0,1},{1,4},{4,5},{5,8},{8,9},{9,12},{12,13},{2,3},{3,6},{6,7},{7,... | collective-permute-start | bytes 2752520 | tf_op jit(solution)/shard_map/ppermute | solution.py:20
  8.9 3.3 %copy.77 = bf16[2,56,1,64,64]{3,4,0,1,2:T(8,128)(2,1)S(1)} copy(bf16[2,56,1,64,64]{4,3,1,0,2:T(8,128)(2,1)} %concatenate.74) | data formatting | bytes 1835008 | tf_op jit(solution)/shard_map/concatenate | solution.py:126
  14.1 3.8 %concatenate.73 = bf16[2,56,1,64,64]{4,3,1,0,2:T(8,128)(2,1)} reshape(bf16[2,56,4096]{2,1,0:T(8,128)(2,1)} %collective-permute-done.1) | data formatting | bytes 1835008 | tf_op jit(solution)/shard_map/concatenate | solution.py:126
  17.9 3.9 %copy.76 = bf16[2,56,1,64,64]{3,4,0,1,2:T(8,128)(2,1)} copy(bf16[2,56,1,64,64]{4,3,1,0,2:T(8,128)(2,1)} %concatenate.73) | data formatting | bytes 1835008 | tf_op jit(solution)/shard_map/concatenate | solution.py:126
  25.9 7.5 %fusion.34 = (bf16[128,1,56,64]{0,3,2,1:T(8,128)(2,1)S(1)}, bf16[128,1,56,64]{0,3,2,1:T(8,128)(2,1)S(1)}) fusion(f32[128,1,56,2,64]{0,4,3,2,1:T(8,128)S(1)} %convolution_bitcast_fusion.6, f32[128,64]{0,1:T(8,128)S(1)} %get-tuple-element.26, f32[128,64]{0,1:T(8,128)S(1)} %get-tuple-element.25, f32[56]{0:T(128)S(1)} %slice.79), kind=kLoop, calls=%fused_computation.81 | loop fusion | flops 4587520 | bytes 5570784 | tf_op jit(solution)/shard_map/concatenate | solution.py:146
  36.3 10.1 %all-to-all-start.1 = ((bf16[128,1,56,128]{3,2,1,0:T(8,128)(2,1)}), bf16[128,1,56,128]{3,2,1,0:T(8,128)(2,1)}, u32[]{:S(2)}, u32[]{:S(2)}) async-start(bf16[128,1,56,128]{3,2,1,0:T(8,128)(2,1)} %copy.84), calls=%async_computation.1 | async-start | bytes 3670016 | tf_op jit(solution)/shard_map/all_to_all | solution.py:180
  53.8 3.3 %concatenate.67 = bf16[2,64,1,64,64]{4,3,1,0,2:T(8,128)(2,1)S(1)} reshape(bf16[2,64,4096]{2,1,0:T(8,128)(2,1)} %collective-permute-done) | data formatting | bytes 2097152 | tf_op jit(solution)/shard_map/concatenate | solution.py:126
  59.8 3.4 %convolution_bitcast_fusion.3 = f32[64,1,2,128,64]{3,4,2,0,1:T(8,128)S(1)} fusion(bf16[2,64,1,64,64]{3,4,0,1,2:T(8,128)(2,1)} %copy.67, bf16[2,64,1,64,64]{3,4,0,1,2:T(8,128)(2,1)} %copy.66, bf16[1,128,2,128]{3,1,2,0:T(8,128)(2,1)S(1)} %get-tuple-element.10, bf16[1,128,2,128]{3,1,2,0:T(8,128)(2,1)S(1)} %get-tuple-element.13), kind=kOutput, calls=%fused_computation.3 | convolution fusion | flops 541327360 | bytes 6422528 | tf_op jit(solution)/shard_map/pkqt,qcfts->cfpks/dot_general | solution.py:129
  65.0 8.6 %fusion.28 = (bf16[128,1,64,64]{0,3,2,1:T(8,128)(2,1)S(1)}, bf16[128,1,64,64]{0,3,2,1:T(8,128)(2,1)S(1)}) fusion(f32[128,1,64,2,64]{0,4,3,2,1:T(8,128)S(1)} %convolution_bitcast_fusion.2, f32[128,64]{0,1:T(8,128)S(1)} %get-tuple-element.26, f32[128,64]{0,1:T(8,128)S(1)} %get-tuple-element.25, f32[64]{0:T(128)S(1)} %bitcast.368), kind=kLoop, calls=%fused_computation.74 | loop fusion | flops 5242880 | bytes 6357248 | tf_op jit(solution)/shard_map/concatenate | solution.py:146
  76.6 11.0 %all-to-all-done.1 = bf16[128,1,56,128]{3,2,1,0:T(8,128)(2,1)} async-done(((bf16[128,1,56,128]{3,2,1,0:T(8,128)(2,1)}), bf16[128,1,56,128]{3,2,1,0:T(8,128)(2,1)}, u32[]{:S(2)}, u32[]{:S(2)}) %all-to-all-start.1) | async-done | bytes 1835040 | tf_op jit(solution)/shard_map/all_to_all | solution.py:180
  87.6 36.7 %all-to-all-start = ((bf16[128,1,64,128]{3,2,1,0:T(8,128)(2,1)}), bf16[128,1,64,128]{3,2,1,0:T(8,128)(2,1)S(1)}, u32[]{:S(2)}, u32[]{:S(2)}) async-start(bf16[128,1,64,128]{3,2,1,0:T(8,128)(2,1)} %copy.74), calls=%async_computation | async-start | bytes 4194304 | tf_op jit(solution)/shard_map/all_to_all | solution.py:180
  128.9 3.9 %reshape.645.refs_1_ = bf16[4,2,56,2048]{3,2,1,0:T(8,128)(2,1)} reshape(bf16[4,1,2,56,16,128]{5,4,3,2,0,1:T(8,128)(2,1)} %copy.85) | data formatting | bytes 3670016 | tf_op jit(solution)/shard_map/reshape | solution.py:185
  132.8 38.2 %all-to-all-done = bf16[128,1,64,128]{3,2,1,0:T(8,128)(2,1)S(1)} async-done(((bf16[128,1,64,128]{3,2,1,0:T(8,128)(2,1)}), bf16[128,1,64,128]{3,2,1,0:T(8,128)(2,1)S(1)}, u32[]{:S(2)}, u32[]{:S(2)}) %all-to-all-start) | async-done | bytes 2097184 | tf_op jit(solution)/shard_map/all_to_all | solution.py:180
  178.1 16.3 %shard_map.56 = bf16[4,112,2048]{2,1,0:T(8,128)(2,1)S(1)} custom-call(s32[1,2048]{1,0:T(1,128)S(1)} %reshape.637.picks_ref, bf16[12,224,240]{2,1,0:T(8,128)(2,1)S(1)} %bitcast.358, bf16[4,2,64,2048]{3,2,1,0:T(8,128)(2,1)S(1)} %reshape.642.refs_0_, bf16[4,2,56,2048]{3,2,1,0:T(8,128)(2,1)S(1)} %copy-done), custom_call_target="tpu_custom_call" | custom-call | flops 10569646080 | bytes 7057408 | tf_op jit(solution)/shard_map/pallas_call | solution.py:101
  196.7 4.5 %all-to-all-start.3 = ((bf16[128,1,56,128]{3,2,1,0:T(8,128)(2,1)}), bf16[128,1,56,128]{3,2,1,0:T(8,128)(2,1)}, u32[]{:S(2)}, u32[]{:S(2)}) async-start(bf16[128,1,56,128]{3,2,1,0:T(8,128)(2,1)} %bitcast.362), calls=%async_computation.3 | async-start | bytes 3670016 | tf_op jit(solution)/shard_map/all_to_all | solution.py:202
  203.2 18.0 %shard_map.55 = bf16[4,128,2048]{2,1,0:T(8,128)(2,1)S(1)} custom-call(s32[1,2048]{1,0:T(1,128)S(1)} %reshape.637.picks_ref, bf16[12,256,240]{2,1,0:T(8,128)(2,1)S(1)} %bitcast.357, bf16[4,2,64,2048]{3,2,1,0:T(8,128)(2,1)S(1)} %reshape.642.refs_0_, bf16[4,2,56,2048]{3,2,1,0:T(8,128)(2,1)S(1)} %copy-done.1), custom_call_target="tpu_custom_call" | custom-call | flops 12079595520 | bytes 7503872 | tf_op jit(solution)/shard_map/pallas_call | solution.py:101
  223.7 19.5 %all-to-all-done.3 = bf16[128,1,56,128]{3,2,1,0:T(8,128)(2,1)} async-done(((bf16[128,1,56,128]{3,2,1,0:T(8,128)(2,1)}), bf16[128,1,56,128]{3,2,1,0:T(8,128)(2,1)}, u32[]{:S(2)}, u32[]{:S(2)}) %all-to-all-start.3) | async-done | bytes 1835040 | tf_op jit(solution)/shard_map/all_to_all | solution.py:202
  243.1 4.3 %all-to-all-start.2 = ((bf16[128,1,64,128]{3,2,1,0:T(8,128)(2,1)}), bf16[128,1,64,128]{3,2,1,0:T(8,128)(2,1)}, u32[]{:S(2)}, u32[]{:S(2)}) async-start(bf16[128,1,64,128]{3,2,1,0:T(8,128)(2,1)} %bitcast.61), calls=%async_computation.2 | async-start | bytes 4194304 | tf_op jit(solution)/shard_map/all_to_all | solution.py:202
  247.5 3.2 %copy.97 = bf16[128,1,56,128]{0,3,2,1:T(8,128)(2,1)S(1)} copy(bf16[128,1,56,128]{3,2,1,0:T(8,128)(2,1)} %all-to-all-done.3) | data formatting | bytes 3670016 | tf_op jit(solution)/shard_map/all_to_all | solution.py:202
  255.1 5.3 %copy.103 = f32[2,56,1,64,64]{4,3,1,0,2:T(8,128)} copy(f32[2,56,1,64,64]{3,4,0,1,2:T(8,128)} %convolution_bitcast_fusion.4) | data formatting | bytes 3670016 | tf_op jit(solution)/shard_map/rupj,cjfpt->rcfut/transpose | solution.py:155
  263.7 31.4 %all-to-all-done.2 = bf16[128,1,64,128]{3,2,1,0:T(8,128)(2,1)} async-done(((bf16[128,1,64,128]{3,2,1,0:T(8,128)(2,1)}), bf16[128,1,64,128]{3,2,1,0:T(8,128)(2,1)}, u32[]{:S(2)}, u32[]{:S(2)}) %all-to-all-start.2) | async-done | bytes 2097184 | tf_op jit(solution)/shard_map/all_to_all | solution.py:202
  295.2 3.3 %copy.88 = bf16[128,1,64,128]{0,3,2,1:T(8,128)(2,1)S(1)} copy(bf16[128,1,64,128]{3,2,1,0:T(8,128)(2,1)} %all-to-all-done.2) | data formatting | bytes 4194304 | tf_op jit(solution)/shard_map/all_to_all | solution.py:202
  302.9 5.7 %copy.94 = f32[2,64,1,64,64]{4,3,1,0,2:T(8,128)} copy(f32[2,64,1,64,64]{3,4,0,1,2:T(8,128)} %convolution_bitcast_fusion) | data formatting | bytes 4194304 | tf_op jit(solution)/shard_map/rupj,cjfpt->rcfut/transpose | solution.py:155
  308.6 3.5 %reshape.649 = f32[2,64,4096]{2,1,0:T(8,128)S(1)} reshape(f32[2,64,1,64,64]{4,3,1,0,2:T(8,128)} %copy.94) | data formatting | bytes 4194304 | tf_op jit(solution)/shard_map/reshape | solution.py:161
  (75 shorter events, 61.4 us)
Async XLA Ops:
  2.0 12.1 %collective-permute-start.1 = (bf16[2,56,4096]{2,1,0:T(8,128)(2,1)S(1)}, bf16[2,56,4096]{2,1,0:T(8,128)(2,1)}, u32[]{:S(2)}, u32[]{:S(2)}) collective-permute-start(bf16[2,56,4096]{2,1,0:T(8,128)(2,1)S(1)} %slice_multiply_fusion.1), channel_id=1, source_target_pairs={{0,1},{1,4},{4,5},{5,8},{8,9},{9,12},{12,13},{2,3},{3,6},{6,7},{7,... | collective-permute-start | bytes 2752520 | tf_op jit(solution)/shard_map/ppermute | solution.py:20
  8.9 3.3 %copy-start.8 = (f32[120]{0:T(128)S(1)}, f32[120]{0:T(128)}, u32[]{:S(2)}) copy-start(f32[120]{0:T(128)} %param.7) | copy-start | bytes 1444
  8.9 5.1 %copy-start.9 = (s32[120]{0:T(128)S(1)}, s32[120]{0:T(128)}, u32[]{:S(2)}) copy-start(s32[120]{0:T(128)} %param.6) | copy-start | bytes 1444
  36.3 10.1 %copy-start.2 = (bf16[2,120,4096]{2,1,0:T(8,128)(2,1)S(1)}, bf16[2,120,4096]{2,1,0:T(8,128)(2,1)}, u32[]{:S(2)}) copy-start(bf16[2,120,4096]{2,1,0:T(8,128)(2,1)} %param.5) | copy-start | bytes 5898244
  36.3 51.3 %all-to-all-start.1 = ((bf16[128,1,56,128]{3,2,1,0:T(8,128)(2,1)}), bf16[128,1,56,128]{3,2,1,0:T(8,128)(2,1)}, u32[]{:S(2)}, u32[]{:S(2)}) async-start(bf16[128,1,56,128]{3,2,1,0:T(8,128)(2,1)} %copy.84), calls=%async_computation.1 | async-start | bytes 3670016 | tf_op jit(solution)/shard_map/all_to_all | solution.py:180
  46.6 7.3 %collective-permute-start = (bf16[2,64,4096]{2,1,0:T(8,128)(2,1)S(1)}, bf16[2,64,4096]{2,1,0:T(8,128)(2,1)}, u32[]{:S(2)}, u32[]{:S(2)}) collective-permute-start(bf16[2,64,4096]{2,1,0:T(8,128)(2,1)S(1)} %slice_multiply_fusion), channel_id=1, source_target_pairs={{0,1},{1,4},{4,5},{5,8},{8,9},{9,12},{12,13},{2,3},{3,6},{6,7},{7,... | collective-permute-start | bytes 3145736 | tf_op jit(solution)/shard_map/ppermute | solution.py:20
  76.6 47.7 %copy-start.7 = (s32[64,16]{0,1:T(8,128)S(1)}, s32[64,16]{0,1:T(8,128)}, u32[]{:S(2)}) copy-start(s32[64,16]{0,1:T(8,128)} %param.9) | copy-start | bytes 12292
  87.6 83.4 %all-to-all-start = ((bf16[128,1,64,128]{3,2,1,0:T(8,128)(2,1)}), bf16[128,1,64,128]{3,2,1,0:T(8,128)(2,1)S(1)}, u32[]{:S(2)}, u32[]{:S(2)}) async-start(bf16[128,1,64,128]{3,2,1,0:T(8,128)(2,1)} %copy.74), calls=%async_computation | async-start | bytes 4194304 | tf_op jit(solution)/shard_map/all_to_all | solution.py:180
  176.6 1.5 copy-start
  196.7 46.5 %all-to-all-start.3 = ((bf16[128,1,56,128]{3,2,1,0:T(8,128)(2,1)}), bf16[128,1,56,128]{3,2,1,0:T(8,128)(2,1)}, u32[]{:S(2)}, u32[]{:S(2)}) async-start(bf16[128,1,56,128]{3,2,1,0:T(8,128)(2,1)} %bitcast.362), calls=%async_computation.3 | async-start | bytes 3670016 | tf_op jit(solution)/shard_map/all_to_all | solution.py:202
  201.2 2.0 copy-start.1
  243.1 52.1 %all-to-all-start.2 = ((bf16[128,1,64,128]{3,2,1,0:T(8,128)(2,1)}), bf16[128,1,64,128]{3,2,1,0:T(8,128)(2,1)}, u32[]{:S(2)}, u32[]{:S(2)}) async-start(bf16[128,1,64,128]{3,2,1,0:T(8,128)(2,1)} %bitcast.61), calls=%async_computation.2 | async-start | bytes 4194304 | tf_op jit(solution)/shard_map/all_to_all | solution.py:202
  247.5 3.2 %copy-start.5 = (bf16[1,64,2,64]{3,1,2,0:T(8,128)(2,1)S(1)}, bf16[1,64,2,64]{3,1,2,0:T(8,128)(2,1)}, u32[]{:S(2)}) copy-start(bf16[1,64,2,64]{3,1,2,0:T(8,128)(2,1)} %get-tuple-element.15) | copy-start | bytes 49156
  247.5 3.2 %copy-start.6 = (bf16[1,64,2,64]{3,1,2,0:T(8,128)(2,1)S(1)}, bf16[1,64,2,64]{3,1,2,0:T(8,128)(2,1)}, u32[]{:S(2)}) copy-start(bf16[1,64,2,64]{3,1,2,0:T(8,128)(2,1)} %get-tuple-element.20) | copy-start | bytes 49156
  251.8 0.8 copy-start.3
  251.8 0.9 copy-start.4

commit v3 on v2

--- a/solution.py
+++ b/solution.py
@@ -71,11 +71,23 @@
 
 def equalise_kernel(parts, picks_ref, weights_ref, *refs):
     out_ref = refs[parts]
-    shares = refs[0].shape[1]
-    pieces = [refs[part][0, share] for share in range(shares) for part in range(parts)]
-    values = jnp.concatenate([piece.astype(jnp.float32) for piece in pieces], axis=0)
+    shares, rows, size, lanes = out_ref.shape
+    values = jnp.concatenate(
+        [
+            jnp.concatenate(
+                [
+                    refs[part][share, row].astype(jnp.float32)
+                    for share in range(shares)
+                    for part in range(parts)
+                ],
+                axis=0,
+            )
+            for row in range(rows)
+        ],
+        axis=1,
+    )
     width = values.shape[1]
-    outputs = out_ref.shape[1]
+    outputs = shares * size
     chosen = jnp.broadcast_to(picks_ref[...], values.shape)
     mixed = jnp.zeros((2 * outputs, width), jnp.float32)
     for block in range(weights_ref.shape[0]):
@@ -83,44 +95,49 @@
         mixed = mixed + jnp.dot(
             weights_ref[block], part, preferred_element_type=jnp.float32
         )
-    lane = lax.broadcasted_iota(jnp.int32, (outputs, 2 * N2), 1)
-    for start in range(0, width, 2 * N2):
-        by_real = mixed[:outputs, start : start + 2 * N2]
-        by_imag = pltpu.roll(mixed[outputs:, start : start + 2 * N2], N2, 1)
+    lane = lax.broadcasted_iota(jnp.int32, (outputs, lanes), 1)
+    for row in range(rows):
+        by_real = mixed[:outputs, row * lanes : (row + 1) * lanes]
+        by_imag = pltpu.roll(mixed[outputs:, row * lanes : (row + 1) * lanes], N2, 1)
         turned = by_real + jnp.where(lane < N2, -by_imag, by_imag)
-        out_ref[0, :, start : start + 2 * N2] = turned.astype(jnp.bfloat16)
-
-
-def equalise(columns, weights, picks):
-    frames, _, _, lanes = columns[0].shape
-    blocks, rows, channels = weights.shape
-    outputs = rows // 2
-    width = math.gcd(lanes, 8 * N2)
-    flops = 2 * frames * lanes * blocks * rows * channels
-    moved = 2 * (weights.size + frames * lanes * (channels + outputs))
+        for share in range(shares):
+            piece = turned[share * size : (share + 1) * size]
+            out_ref[share, row] = piece.astype(jnp.bfloat16)
+
+
+def equalise(columns, weights, picks, size):
+    times, shares, rows, frames, _, lanes = columns[0].shape
+    blocks, outputs, channels = weights.shape
+    step = math.gcd(rows, 4)
+    flops = 2 * times * frames * rows * lanes * blocks * outputs * channels
+    moved = 2 * (weights.size + times * frames * rows * lanes * (channels + outputs // 2))
+
+    def spec(channels_part):
+        return pl.BlockSpec(
+            (None, shares, step, None, channels_part, lanes),
+            lambda t, f, i: (t, 0, i, f, 0, 0),
+        )
+
     return pl.pallas_call(
         functools.partial(equalise_kernel, len(columns)),
-        grid=(frames, lanes // width),
+        grid=(times, frames, rows // step),
         in_specs=[
-            pl.BlockSpec((1, width), lambda m, i: (0, i)),
-            pl.BlockSpec((blocks, rows, channels), lambda m, i: (0, 0, 0)),
+            pl.BlockSpec((1, step * lanes), lambda t, f, i: (0, i)),
+            pl.BlockSpec((blocks, outputs, channels), lambda t, f, i: (0, 0, 0)),
         ]
-        + [
-            pl.BlockSpec((1,) + part.shape[1:3] + (width,), lambda m, i: (m, 0, 0, i))
-            for part in columns
-        ],
-        out_specs=pl.BlockSpec((1, outputs, width), lambda m, i: (m, 0, i)),
-        out_shape=jax.ShapeDtypeStruct((frames, outputs, lanes), jnp.bfloat16),
+        + [spec(part.shape[4]) for part in columns],
+        out_specs=spec(size),
+        out_shape=jax.ShapeDtypeStruct(
+            (times, shares, rows, frames, size, lanes), jnp.bfloat16
+        ),
         cost_estimate=pl.CostEstimate(flops=flops, bytes_accessed=moved, transcendentals=0),
         compiler_params=pltpu.CompilerParams(vmem_limit_bytes=40 * 1024 * 1024),
     )(picks, weights, *columns)
 
 
-def to_bins(signal, channel_mask, dispersion, forward_first, forward_second):
-    channels = signal.shape[1]
-    frame_count = signal.shape[2] // TAPS
-    masked = signal * channel_mask.astype(jnp.bfloat16)[None, :, None]
-    tail_in = from_behind(masked[:, :, -TAPS:], ("tm", "sub"), 1)
+def to_bins(masked, tail_in, dispersion, forward_first, forward_second):
+    channels = masked.shape[1]
+    frame_count = masked.shape[2] // TAPS
     own_halves = masked.reshape(2, channels, frame_count, TAPS)
     previous = jnp.concatenate([tail_in[:, :, None], own_halves[:, :, :-1]], axis=2)
     frames = jnp.concatenate([previous, own_halves], axis=3).reshape(
@@ -173,17 +190,18 @@
     forward = (dft_table(N1, False), dft_table(N2, False))
     inverse = (dft_table(N1, True), dft_table(N2, True))
     columns = []
-    for low, high in parts:
-        dispersed = to_bins(
-            signal[:, low:high], channel_mask[low:high], dispersion[low:high], *forward
-        )
+    mask_half = channel_mask.astype(jnp.bfloat16)
+    masked = [signal[:, low:high] * mask_half[None, low:high, None] for low, high in parts]
+    tails = [from_behind(part[:, :, -TAPS:], ("tm", "sub"), 1) for part in masked]
+    for index, (low, high) in enumerate(parts):
+        dispersed = to_bins(masked[index], tails[index], dispersion[low:high], *forward)
+        dispersed, tails = lax.optimization_barrier((dispersed, tails))
         by_bins = lax.all_to_all(
             dispersed, ("tm", "chan"), split_axis=0, concat_axis=0, tiled=True
         )
-        grid = by_bins.reshape(tm_count, chan_count, bins_rows, frame_count, high - low, 2 * N2)
         columns.append(
-            jnp.transpose(grid, (0, 3, 1, 4, 2, 5)).reshape(
-                tm_count * frame_count, chan_count, high - low, bins_rows * 2 * N2
+            by_bins.reshape(
+                tm_count, chan_count, bins_rows, frame_count, high - low, 2 * N2
             )
         )
     picks = jnp.broadcast_to(bin_block.T[:, None, :], (bins_rows, 2, N2)).reshape(1, -1)
@@ -193,10 +211,7 @@
     for low, high in parts:
         rows = 2 * chan_count * (high - low)
         mine = weights[:, :, :, low:high].reshape(blocks, rows, channels)
-        equalised = equalise(columns, mine, picks).reshape(
-            tm_count, frame_count, chan_count, high - low, bins_rows, 2 * N2
-        )
-        equalised = jnp.transpose(equalised, (0, 2, 4, 1, 3, 5)).reshape(
+        equalised = equalise(columns, mine, picks, high - low).reshape(
             N1, frame_count, high - low, 2 * N2
         )
         returned = lax.all_to_all(

time: 315 us -> 309 us (0.981)
  waiting for transfers between devices: 100 us -> 138 us
  starting transfers between devices: 61.3 us -> 24.4 us
  local copies, waits for them, and re-layouts: 77.2 us -> 65.3 us
  other arithmetic: 26.5 us -> 30 us
    all_to_all x2, starting transfers between devices: 46.8 us -> 7.53 us  [on_device(): lax.all_to_all(dispersed, ('tm', 'chan'), split_axis=0, concat_axis=0, ti...]
    all_to_all x2, waiting for transfers between devices: 49.2 us -> 85.5 us  [on_device(): lax.all_to_all(dispersed, ('tm', 'chan'), split_axis=0, concat_axis=0, ti...]
    reshape x4 -> x0, local copies, waits for them, and re-layouts: 10.2 us -> none  [the longest x2 6.68 us: on_device(): jnp.transpose(grid, (0, 3, 1, 4, 2, 5))]
    optimization_barrier x0 -> x2, local copies, waits for them, and re-layouts: none -> 6.8 us  [on_device(): dispersed, tails = lax.optimization_barrier((dispersed, tails))]
    transpose x2 -> x0, local copies, waits for them, and re-layouts: 5.79 us -> none  [on_device(): jnp.transpose(grid, (0, 3, 1, 4, 2, 5))]
    concatenate x2 -> x0, local copies, waits for them, and re-layouts: 5.56 us -> none  [to_bins(): jnp.concatenate([real_s * cos_disp - imag_s * sin_disp, real_s * sin_disp...]
  transfers between devices with their start and end apart: 6 -> 6, of which waited for: 4 -> 4; matrix products, arithmetic and copies ran while one was open for 21% -> 20% of each run, Pallas kernels for 6% -> 6%
where the time goes in v3:
time: 309 us; the launch traced here: 308 us
  waiting for transfers between devices  138 us (45%)
  local copies, waits for them, and re-layouts  65.3 us (21%)
  Pallas kernels  35.2 us (11%)
  other arithmetic  30 us (10%)
  starting transfers between devices  24.4 us (8%)
  matrix products  14 us (5%)
    all_to_all x2, waiting for transfers between devices, on_device(): lax.all_to_all(dispersed, ('tm', 'chan'), split_axis=0, concat_axis=0, ti...  85.5 us
    all_to_all x2, waiting for transfers between devices, on_device(): lax.all_to_all(equalised, ('tm', 'chan'), split_axis=0, concat_axis=0, ti...  52.8 us
    pallas_call x2, Pallas kernels, equalise(): pl.pallas_call(functools.partial(equalise_kernel, len(columns)), grid=(ti...  35.2 us
    concatenate x8, local copies, waits for them, and re-layouts, to_bins(): jnp.concatenate([previous, own_halves], axis=3)  26.4 us
    concatenate x4, other arithmetic, to_bins(): jnp.concatenate([real_s * cos_disp - imag_s * sin_disp, real_s * sin_disp...  17.8 us
    transpose x2, local copies, waits for them, and re-layouts, from_bins(): jnp.einsum('rupj,cjfpt->rcfut', inverse_first[:, N1 // 2:], restored, pre...  11 us
    all_to_all x2, starting transfers between devices, on_device(): lax.all_to_all(equalised, ('tm', 'chan'), split_axis=0, concat_axis=0, ti...  9.02 us
    ppermute x2, starting transfers between devices, from_behind(): return lax.ppermute(value, axis, pairs)  7.89 us
  transfers between devices with their start and end apart: 6, of which 4 were waited for; matrix products, arithmetic and copies ran while one was open for 20% of the time, Pallas kernels for 6%

profile of v3, /device:TPU:0, one launch (start us, length us, event | category | flops | bytes accessed | tf_op | source)
XLA Modules:
  0.0 307.7 jit_solution(71156608850633647)
XLA Ops:
  2.0 3.4 %collective-permute-start = (bf16[2,64,4096]{2,1,0:T(8,128)(2,1)S(1)}, bf16[2,64,4096]{2,1,0:T(8,128)(2,1)}, u32[]{:S(2)}, u32[]{:S(2)}) collective-permute-start(bf16[2,64,4096]{2,1,0:T(8,128)(2,1)S(1)} %slice_multiply_fusion), channel_id=1, source_target_pairs={{0,1},{1,4},{4,5},{5,8},{8,9},{9,12},{12,13},{2,3},{3,6},{6,7},{7,... | collective-permute-start | bytes 3145736 | tf_op jit(solution)/shard_map/ppermute | solution.py:20
  7.7 4.5 %collective-permute-start.1 = (bf16[2,56,4096]{2,1,0:T(8,128)(2,1)}, bf16[2,56,4096]{2,1,0:T(8,128)(2,1)}, u32[]{:S(2)}, u32[]{:S(2)}) collective-permute-start(bf16[2,56,4096]{2,1,0:T(8,128)(2,1)} %slice_multiply_fusion.1), channel_id=1, source_target_pairs={{0,1},{1,4},{4,5},{5,8},{8,9},{9,12},{12,13},{2,3},{3,6},{6,7},{7,... | collective-permute-start | bytes 2752520 | tf_op jit(solution)/shard_map/ppermute | solution.py:20
  14.5 3.8 %concatenate.74 = bf16[2,56,1,64,64]{4,3,1,0,2:T(8,128)(2,1)} reshape(bf16[2,56,4096]{2,1,0:T(8,128)(2,1)} %slice_multiply_fusion.1) | data formatting | bytes 1835008 | tf_op jit(solution)/shard_map/concatenate | solution.py:143
  21.0 3.9 %copy.74 = bf16[2,56,1,64,64]{3,4,0,1,2:T(8,128)(2,1)} copy(bf16[2,56,1,64,64]{4,3,1,0,2:T(8,128)(2,1)} %concatenate.74) | data formatting | bytes 1835008 | tf_op jit(solution)/shard_map/concatenate | solution.py:143
  33.3 3.4 %convolution_bitcast_fusion.3 = f32[64,1,2,128,64]{3,4,2,0,1:T(8,128)S(1)} fusion(bf16[2,64,1,64,64]{3,4,0,1,2:T(8,128)(2,1)} %copy.65, bf16[2,64,1,64,64]{3,4,0,1,2:T(8,128)(2,1)} %copy.64, bf16[1,128,2,128]{3,1,2,0:T(8,128)(2,1)S(1)} %get-tuple-element.16, bf16[1,128,2,128]{3,1,2,0:T(8,128)(2,1)S(1)} %get-tuple-element.19), kind=kOutput, calls=%fused_computation.3 | convolution fusion | flops 541327360 | bytes 6422528 | tf_op jit(solution)/shard_map/pkqt,qcfts->cfpks/dot_general | solution.py:146
  38.6 8.6 %fusion.28 = (bf16[128,1,64,64]{0,3,2,1:T(8,128)(2,1)S(1)}, bf16[128,1,64,64]{0,3,2,1:T(8,128)(2,1)S(1)}) fusion(f32[128,1,64,2,64]{0,4,3,2,1:T(8,128)S(1)} %convolution_bitcast_fusion.2, f32[128,64]{0,1:T(8,128)S(1)} %get-tuple-element.28, f32[128,64]{0,1:T(8,128)S(1)} %get-tuple-element.27, f32[64]{0:T(128)S(1)} %bitcast.342), kind=kLoop, calls=%fused_computation.74 | loop fusion | flops 5242880 | bytes 6357248 | tf_op jit(solution)/shard_map/concatenate | solution.py:163
  48.7 3.8 %concatenate.73 = bf16[2,56,1,64,64]{4,3,1,0,2:T(8,128)(2,1)} reshape(bf16[2,56,4096]{2,1,0:T(8,128)(2,1)} %collective-permute-done.1) | data formatting | bytes 1835008 | tf_op jit(solution)/shard_map/concatenate | solution.py:143
  52.5 4.0 %copy.73 = bf16[2,56,1,64,64]{3,4,0,1,2:T(8,128)(2,1)} copy(bf16[2,56,1,64,64]{4,3,1,0,2:T(8,128)(2,1)} %concatenate.73) | data formatting | bytes 1835008 | tf_op jit(solution)/shard_map/concatenate | solution.py:143
  60.6 7.5 %fusion.34 = (bf16[128,1,56,64]{0,3,2,1:T(8,128)(2,1)S(1)}, bf16[128,1,56,64]{0,3,2,1:T(8,128)(2,1)S(1)}) fusion(f32[128,1,56,2,64]{0,4,3,2,1:T(8,128)S(1)} %convolution_bitcast_fusion.6, f32[128,64]{0,1:T(8,128)S(1)} %get-tuple-element.28, f32[128,64]{0,1:T(8,128)S(1)} %get-tuple-element.27, f32[56]{0:T(128)S(1)} %slice.83), kind=kLoop, calls=%fused_computation.81 | loop fusion | flops 4587520 | bytes 5570784 | tf_op jit(solution)/shard_map/concatenate | solution.py:163
  71.0 3.9 %all-to-all-start.1 = ((bf16[128,1,56,128]{3,2,1,0:T(8,128)(2,1)}), bf16[128,1,56,128]{3,2,1,0:T(8,128)(2,1)S(1)}, u32[]{:S(2)}, u32[]{:S(2)}) async-start(bf16[128,1,56,128]{3,2,1,0:T(8,128)(2,1)} %copy.81), calls=%async_computation.1 | async-start | bytes 3670016 | tf_op jit(solution)/shard_map/all_to_all | solution.py:199
  74.9 4.1 %copy.72 = bf16[128,1,64,128]{3,2,1,0:T(8,128)(2,1)} copy(bf16[128,1,64,128]{0,3,2,1:T(8,128)(2,1)} %pad_maximum_fusion) | data formatting | bytes 4194304 | tf_op jit(solution)/shard_map/optimization_barrier | solution.py:198
  79.0 38.7 %all-to-all-done.1 = bf16[128,1,56,128]{3,2,1,0:T(8,128)(2,1)S(1)} async-done(((bf16[128,1,56,128]{3,2,1,0:T(8,128)(2,1)}), bf16[128,1,56,128]{3,2,1,0:T(8,128)(2,1)S(1)}, u32[]{:S(2)}, u32[]{:S(2)}) %all-to-all-start.1) | async-done | bytes 1835040 | tf_op jit(solution)/shard_map/all_to_all | solution.py:199
  118.9 3.6 %all-to-all-start = ((bf16[128,1,64,128]{3,2,1,0:T(8,128)(2,1)}), bf16[128,1,64,128]{3,2,1,0:T(8,128)(2,1)S(1)}, u32[]{:S(2)}, u32[]{:S(2)}) async-start(bf16[128,1,64,128]{3,2,1,0:T(8,128)(2,1)} %copy.72), calls=%async_computation | async-start | bytes 4194304 | tf_op jit(solution)/shard_map/all_to_all | solution.py:199
  124.1 46.9 %all-to-all-done = bf16[128,1,64,128]{3,2,1,0:T(8,128)(2,1)S(1)} async-done(((bf16[128,1,64,128]{3,2,1,0:T(8,128)(2,1)}), bf16[128,1,64,128]{3,2,1,0:T(8,128)(2,1)S(1)}, u32[]{:S(2)}, u32[]{:S(2)}) %all-to-all-start) | async-done | bytes 2097184 | tf_op jit(solution)/shard_map/all_to_all | solution.py:199
  172.4 16.5 %shard_map.56 = bf16[4,2,16,1,56,128]{5,4,3,2,1,0:T(8,128)(2,1)S(1)} custom-call(s32[1,2048]{1,0:T(1,128)S(1)} %reshape.625.picks_ref, bf16[12,224,240]{2,1,0:T(8,128)(2,1)S(1)} %bitcast.336, bf16[4,2,16,1,64,128]{5,4,3,2,1,0:T(8,128)(2,1)S(1)} %bitcast.330, bf16[4,2,16,1,56,128]{5,4,3,2,1,0:T(8,128)(2,1)S(1)} %bitcast.332), custom_call_target="tpu_custom_call" | custom-call | flops 10569646080 | bytes 7057408 | tf_op jit(solution)/shard_map/pallas_call | solution.py:121
  190.1 4.3 %all-to-all-start.3 = ((bf16[128,1,56,128]{3,2,1,0:T(8,128)(2,1)}), bf16[128,1,56,128]{3,2,1,0:T(8,128)(2,1)}, u32[]{:S(2)}, u32[]{:S(2)}) async-start(bf16[128,1,56,128]{3,2,1,0:T(8,128)(2,1)} %bitcast.334), calls=%async_computation.3 | async-start | bytes 3670016 | tf_op jit(solution)/shard_map/all_to_all | solution.py:217
  196.4 18.8 %shard_map.55 = bf16[4,2,16,1,64,128]{5,4,3,2,1,0:T(8,128)(2,1)} custom-call(s32[1,2048]{1,0:T(1,128)S(1)} %reshape.625.picks_ref, bf16[12,256,240]{2,1,0:T(8,128)(2,1)S(1)} %bitcast.335, bf16[4,2,16,1,64,128]{5,4,3,2,1,0:T(8,128)(2,1)S(1)} %bitcast.331, bf16[4,2,16,1,56,128]{5,4,3,2,1,0:T(8,128)(2,1)S(1)} %bitcast.333), custom_call_target="tpu_custom_call" | custom-call | flops 12079595520 | bytes 7503872 | tf_op jit(solution)/shard_map/pallas_call | solution.py:121
  215.2 21.5 %all-to-all-done.3 = bf16[128,1,56,128]{3,2,1,0:T(8,128)(2,1)} async-done(((bf16[128,1,56,128]{3,2,1,0:T(8,128)(2,1)}), bf16[128,1,56,128]{3,2,1,0:T(8,128)(2,1)}, u32[]{:S(2)}, u32[]{:S(2)}) %all-to-all-start.3) | async-done | bytes 1835040 | tf_op jit(solution)/shard_map/all_to_all | solution.py:217
  236.7 4.7 %all-to-all-start.2 = ((bf16[128,1,64,128]{3,2,1,0:T(8,128)(2,1)}), bf16[128,1,64,128]{3,2,1,0:T(8,128)(2,1)}, u32[]{:S(2)}, u32[]{:S(2)}) async-start(bf16[128,1,64,128]{3,2,1,0:T(8,128)(2,1)} %bitcast.58), calls=%async_computation.2 | async-start | bytes 4194304 | tf_op jit(solution)/shard_map/all_to_all | solution.py:217
  249.1 5.3 %copy.97 = f32[2,56,1,64,64]{4,3,1,0,2:T(8,128)} copy(f32[2,56,1,64,64]{3,4,0,1,2:T(8,128)} %convolution_bitcast_fusion.4) | data formatting | bytes 3670016 | tf_op jit(solution)/shard_map/rupj,cjfpt->rcfut/transpose | solution.py:172
  257.8 31.3 %all-to-all-done.2 = bf16[128,1,64,128]{3,2,1,0:T(8,128)(2,1)} async-done(((bf16[128,1,64,128]{3,2,1,0:T(8,128)(2,1)}), bf16[128,1,64,128]{3,2,1,0:T(8,128)(2,1)}, u32[]{:S(2)}, u32[]{:S(2)}) %all-to-all-start.2) | async-done | bytes 2097184 | tf_op jit(solution)/shard_map/all_to_all | solution.py:217
  289.1 3.3 %copy.83 = bf16[128,1,64,128]{0,3,2,1:T(8,128)(2,1)S(1)} copy(bf16[128,1,64,128]{3,2,1,0:T(8,128)(2,1)} %all-to-all-done.2) | data formatting | bytes 4194304 | tf_op jit(solution)/shard_map/all_to_all | solution.py:217
  296.8 5.7 %copy.89 = f32[2,64,1,64,64]{4,3,1,0,2:T(8,128)} copy(f32[2,64,1,64,64]{3,4,0,1,2:T(8,128)} %convolution_bitcast_fusion) | data formatting | bytes 4194304 | tf_op jit(solution)/shard_map/rupj,cjfpt->rcfut/transpose | solution.py:172
  302.5 3.5 %reshape.634 = f32[2,64,4096]{2,1,0:T(8,128)S(1)} reshape(f32[2,64,1,64,64]{4,3,1,0,2:T(8,128)} %copy.89) | data formatting | bytes 4194304 | tf_op jit(solution)/shard_map/reshape | solution.py:178
  (73 shorter events, 52.4 us)
Async XLA Ops:
  2.0 25.4 %collective-permute-start = (bf16[2,64,4096]{2,1,0:T(8,128)(2,1)S(1)}, bf16[2,64,4096]{2,1,0:T(8,128)(2,1)}, u32[]{:S(2)}, u32[]{:S(2)}) collective-permute-start(bf16[2,64,4096]{2,1,0:T(8,128)(2,1)S(1)} %slice_multiply_fusion), channel_id=1, source_target_pairs={{0,1},{1,4},{4,5},{5,8},{8,9},{9,12},{12,13},{2,3},{3,6},{6,7},{7,... | collective-permute-start | bytes 3145736 | tf_op jit(solution)/shard_map/ppermute | solution.py:20
  7.7 41.0 %collective-permute-start.1 = (bf16[2,56,4096]{2,1,0:T(8,128)(2,1)}, bf16[2,56,4096]{2,1,0:T(8,128)(2,1)}, u32[]{:S(2)}, u32[]{:S(2)}) collective-permute-start(bf16[2,56,4096]{2,1,0:T(8,128)(2,1)} %slice_multiply_fusion.1), channel_id=1, source_target_pairs={{0,1},{1,4},{4,5},{5,8},{8,9},{9,12},{12,13},{2,3},{3,6},{6,7},{7,... | collective-permute-start | bytes 2752520 | tf_op jit(solution)/shard_map/ppermute | solution.py:20
  21.0 3.9 %copy-start.10 = (f32[120]{0:T(128)S(1)}, f32[120]{0:T(128)}, u32[]{:S(2)}) copy-start(f32[120]{0:T(128)} %param.7) | copy-start | bytes 1444
  52.5 4.0 %copy-start.4 = (bf16[2,56,1,64,64]{3,4,0,1,2:T(8,128)(2,1)S(1)}, bf16[2,56,1,64,64]{3,4,0,1,2:T(8,128)(2,1)}, u32[]{:S(2)}) copy-start(bf16[2,56,1,64,64]{3,4,0,1,2:T(8,128)(2,1)} %copy.74) | copy-start | bytes 2752516
  71.0 46.7 %all-to-all-start.1 = ((bf16[128,1,56,128]{3,2,1,0:T(8,128)(2,1)}), bf16[128,1,56,128]{3,2,1,0:T(8,128)(2,1)S(1)}, u32[]{:S(2)}, u32[]{:S(2)}) async-start(bf16[128,1,56,128]{3,2,1,0:T(8,128)(2,1)} %copy.81), calls=%async_computation.1 | async-start | bytes 3670016 | tf_op jit(solution)/shard_map/all_to_all | solution.py:199
  79.0 43.5 %copy-start.9 = (s32[64,16]{0,1:T(8,128)S(1)}, s32[64,16]{0,1:T(8,128)}, u32[]{:S(2)}) copy-start(s32[64,16]{0,1:T(8,128)} %param.9) | copy-start | bytes 12292
  117.6 1.2 copy-start
  118.9 52.1 %all-to-all-start = ((bf16[128,1,64,128]{3,2,1,0:T(8,128)(2,1)}), bf16[128,1,64,128]{3,2,1,0:T(8,128)(2,1)S(1)}, u32[]{:S(2)}, u32[]{:S(2)}) async-start(bf16[128,1,64,128]{3,2,1,0:T(8,128)(2,1)} %copy.72), calls=%async_computation | async-start | bytes 4194304 | tf_op jit(solution)/shard_map/all_to_all | solution.py:199
  170.9 1.5 copy-start.1
  188.9 1.2 copy-start.3
  190.1 46.5 %all-to-all-start.3 = ((bf16[128,1,56,128]{3,2,1,0:T(8,128)(2,1)}), bf16[128,1,56,128]{3,2,1,0:T(8,128)(2,1)}, u32[]{:S(2)}, u32[]{:S(2)}) async-start(bf16[128,1,56,128]{3,2,1,0:T(8,128)(2,1)} %bitcast.334), calls=%async_computation.3 | async-start | bytes 3670016 | tf_op jit(solution)/shard_map/all_to_all | solution.py:217
  194.4 2.0 copy-start.2
  236.7 4.7 %copy-start.11 = (s32[120]{0:T(128)S(1)}, s32[120]{0:T(128)}, u32[]{:S(2)}) copy-start(s32[120]{0:T(128)} %param.6) | copy-start | bytes 1444
  236.7 52.4 %all-to-all-start.2 = ((bf16[128,1,64,128]{3,2,1,0:T(8,128)(2,1)}), bf16[128,1,64,128]{3,2,1,0:T(8,128)(2,1)}, u32[]{:S(2)}, u32[]{:S(2)}) async-start(bf16[128,1,64,128]{3,2,1,0:T(8,128)(2,1)} %bitcast.58), calls=%async_computation.2 | async-start | bytes 4194304 | tf_op jit(solution)/shard_map/all_to_all | solution.py:217
  241.4 3.3 %copy-start.7 = (bf16[1,64,2,64]{3,1,2,0:T(8,128)(2,1)S(1)}, bf16[1,64,2,64]{3,1,2,0:T(8,128)(2,1)}, u32[]{:S(2)}) copy-start(bf16[1,64,2,64]{3,1,2,0:T(8,128)(2,1)} %get-tuple-element.21) | copy-start | bytes 49156
  241.4 3.3 %copy-start.8 = (bf16[1,64,2,64]{3,1,2,0:T(8,128)(2,1)S(1)}, bf16[1,64,2,64]{3,1,2,0:T(8,128)(2,1)}, u32[]{:S(2)}) copy-start(bf16[1,64,2,64]{3,1,2,0:T(8,128)(2,1)} %get-tuple-element.26) | copy-start | bytes 49156
  245.8 0.8 copy-start.5
  245.8 0.9 copy-start.6
